TPU v7x, 256 devices: a whole 4x4x8 slice. The times are simulated.
256 devices in a mesh: cell: 8 (over x, core), tm: 32 (over y, z).
Axes of the slice: x: 4, y: 4, z: 8, core: 2. Of those that a mesh axis runs over, the one named last changes fastest.
Arguments:
- state: bfloat16 [8192, 131072], P('tm', 'cell'), may hold values from -120 to 120, as said below
- range_test: bfloat16 [8192, 128], P('tm'), may hold values from -0.0625 to 0.0625
- corange_test: bfloat16 [256, 131072], P(None, 'cell'), may hold values from -0.015625 to 0.015625
Outputs:
- basis: float32 [131072, 128], P(('cell', 'tm'))
- corange: float32 [256, 8192], P(None, 'tm')
Inputs may be any that keep to these rules, and one draw needn't show every extreme that they name: state varies from cell to cell in scale.
All inputs are finite; a program needn't handle non-finite values.
Results may differ from a plain program's by a relative error of at most 0.015.
Values may be sent and summed in bfloat16 or wider, within the bound.
A program may use at most 128 MiB of HBM per device.

v0:
```python
import jax
import jax.numpy as jnp
from jax import lax
from jax.sharding import PartitionSpec as P


def on_device(state, range_test, corange_test):
    parts = lax.axis_size("tm")
    share = state.shape[1] // parts
    summed = lax.psum(
        lax.dot_general(
            state, range_test, (((0,), (0,)), ((), ())), preferred_element_type=jnp.float32
        ),
        "tm",
    )
    sketch = lax.dynamic_slice_in_dim(summed, lax.axis_index("tm") * share, share, 0)
    corange_part = lax.dot_general(
        corange_test, state, (((1,), (1,)), ((), ())), preferred_element_type=jnp.float32
    )
    gram_part = jnp.dot(sketch.T, sketch, precision=lax.Precision.HIGHEST)
    corange = lax.psum(corange_part, "cell")
    gram = lax.psum(gram_part, ("cell", "tm"))
    lower = jnp.linalg.cholesky(gram)
    solved = lax.linalg.triangular_solve(
        lower, sketch, left_side=False, lower=True, transpose_a=True
    )
    total_cells = state.shape[1] * lax.axis_size("cell")
    basis = solved * jnp.sqrt(jnp.float32(total_cells))
    return (basis, corange)


def solution(mesh):
    return jax.shard_map(
        on_device,
        mesh=mesh,
        in_specs=(P("tm", "cell"), P("tm", None), P(None, "cell")),
        out_specs=(P(("cell", "tm"), None), P(None, "tm")),
        check_vma=False,
    )
```

profile of v0, /device:TPU:1, one launch (start us, length us, event | category | flops | bytes accessed | tf_op | source)
XLA Modules:
  0.0 545.6 jit_solution(167367968662751043)
XLA Ops:
  7.2 0.0 copy-start
  7.2 0.0 all-reduce.4.cloned.1.call-start
  7.2 0.8 copy-done
  8.0 9.0 %fusion.8 = f32[16384,128]{1,0:T(8,128)} fusion(bf16[256,16384]{1,0:T(8,128)(2,1)} %param.3, bf16[256,128]{1,0:T(8,128)(2,1)S(1)} %copy-done), kind=kOutput, calls=%fused_computation.15 | convolution fusion | flops 1073741824 | bytes 16842752 | tf_op jit(solution)/shard_map/dot_general | solution.py:11
  17.0 0.0 all-reduce.4.cloned.1.call-update
  17.0 0.0 all-reduce.6.cloned.1.call-start
  17.1 215.5 %all-reduce.4.cloned.1.call-done = f32[16384,128]{1,0:T(8,128)} async-done(((f32[16384,128]{1,0:T(8,128)}), f32[16384,128]{1,0:T(8,128)}) %all-reduce.4.cloned.1.call-update) | async-done | bytes 8388624 | tf_op jit(solution)/shard_map/psum | solution.py:10
  232.6 2.2 fusion.1
  234.8 0.0 all-reduce.6.cloned.1.call-update
  234.9 0.2 all-reduce.8.cloned.1.call-start
  235.1 8.8 %fusion.9 = f32[256,256]{1,0:T(8,128)} fusion(bf16[256,16384]{1,0:T(8,128)(2,1)} %param.5, bf16[256,16384]{1,0:T(8,128)(2,1)} %param.3), kind=kOutput, calls=%fused_computation.16 | convolution fusion | flops 2147483648 | bytes 17039360 | tf_op jit(solution)/shard_map/dot_general | solution.py:17
  243.9 0.0 all-reduce.8.cloned.1.call-update
  244.0 231.4 %all-reduce.6.cloned.1.call-done = f32[128,128]{0,1:T(8,128)} async-done(((f32[128,128]{0,1:T(8,128)}), f32[128,128]{0,1:T(8,128)}) %all-reduce.6.cloned.1.call-update) | async-done | bytes 65552 | tf_op jit(solution)/shard_map/psum | solution.py:22
  475.4 0.9 copy.6
  476.3 0.9 fusion.5
  477.2 11.7 %cholesky.16 = f32[128,128]{1,0:T(8,128)S(1)} custom-call(f32[128,128]{1,0:T(8,128)S(1)} %fusion.5), custom_call_target="Cholesky" | custom-call | tf_op jit(solution)/shard_map/jit(cholesky)/cholesky | solution.py:23
  488.9 0.6 compare_reduce_fusion
  489.6 0.7 fusion.3
  490.2 9.8 %custom-call.6 = f32[1,128,128]{1,2,0:T(8,128)S(1)} custom-call(f32[1,128,128]{2,1,0:T(8,128)S(1)} %fusion.3), custom_call_target="InvertDiagBlocksLowerTriangular" | custom-call | tf_op jit(solution)/shard_map/triangular_solve | solution.py:24
  500.1 2.0 convolution_multiply_fusion
  502.1 35.3 %all-reduce.8.cloned.1.call-done = f32[256,256]{1,0:T(8,128)} async-done(((f32[256,256]{1,0:T(8,128)}), f32[256,256]{1,0:T(8,128)}) %all-reduce.8.cloned.1.call-update) | async-done | bytes 262160 | tf_op jit(solution)/shard_map/psum | solution.py:21
  537.4 1.7 copy.11
  (1 shorter events, 0.0 us)
Async XLA Ops:
  7.2 0.8 copy-start
  7.2 225.4 %all-reduce.4.cloned.1.call-start = ((), (), s32[]{:S(2)}) async-start(), calls=%async_computation | async-start | bytes 16777216 | tf_op jit(solution)/shard_map/psum | solution.py:10
  17.0 458.4 %all-reduce.6.cloned.1.call-start = ((), (), s32[]{:S(2)}) async-start(), calls=%async_computation.1 | async-start | bytes 131072 | tf_op jit(solution)/shard_map/psum | solution.py:22
  234.9 302.5 %all-reduce.8.cloned.1.call-start = ((), (), s32[]{:S(2)}) async-start(), calls=%async_computation.2 | async-start | bytes 524288 | tf_op jit(solution)/shard_map/psum | solution.py:21
Sparse Core Ops, SparseCore 0:
  17.2 215.3 all-reduce.3
  238.7 236.6 all-reduce.5
  478.3 59.0 all-reduce.7
where the time goes:
time: 547 us; the launch traced here: 546 us
  waiting for transfers between devices  482 us (88%)
  other arithmetic  23.7 us (4%)
  matrix products  22.1 us (4%)
  between operations  13.8 us (3%)
    psum x1, waiting for transfers between devices, on_device(): gram = lax.psum(gram_part, ('cell', 'tm'))  231 us
    psum x1, waiting for transfers between devices, on_device(): lax.psum(lax.dot_general(state, range_test, (((0,), (0,)), ((), ())), pre...  216 us
    psum x1, waiting for transfers between devices, on_device(): corange = lax.psum(corange_part, 'cell')  35.3 us
    another operation x3, other arithmetic, on_device(): lower = jnp.linalg.cholesky(gram)  12.4 us
  transfers between devices with their start and end apart: 3, of which 3 were waited for; matrix products, arithmetic and copies ran while one was open for 7% of the time, Pallas kernels for 0%

commit v1 on v0

v1 whole, which is shorter than its diff:
```python
import functools

import jax
import jax.numpy as jnp
from jax import lax
from jax.experimental import pallas as pl
from jax.experimental.pallas import tpu as pltpu
from jax.sharding import PartitionSpec as P

MESH = pl.DeviceIdType.MESH
F32, BF16 = jnp.float32, jnp.bfloat16
NY, NZ, NC = 4, 8, 8
RANK, STEPS, OWN, HALF = 128, 256, 512, 256
A = 80
SCALE = 32768.0
ORDER = (4, 3, 5, 2, 6, 1, 7, 0)


def encode(x):
    s = x * x
    return (s * x * jnp.abs(x)).astype(BF16)


def decode(y):
    y = y.astype(F32)
    r = lax.rsqrt(lax.rsqrt(jnp.maximum(jnp.abs(y), 1.2e-38)))
    return jnp.where(y < 0, -r, r)


def span(h):
    return pl.ds(h * HALF, HALF)


class Ring:
    def __init__(self, lead, snd, rcv, ssem, rsem, plus, minus, targets):
        self.lead, self.snd, self.rcv = lead, snd, rcv
        self.ssem, self.rsem = ssem, rsem
        self.ids = {1: plus, -1: minus}
        self.targets = targets

    def copy(self, m):
        i = self.lead + (m,)
        return pltpu.make_async_remote_copy(
            self.snd.at[i], self.rcv.at[i], self.ssem.at[i], self.rsem.at[i],
            device_id=self.ids[self.targets[m]], device_id_type=MESH,
        )

    def put(self, m, value):
        self.snd[self.lead + (m,)] = encode(value)

    def send(self, m):
        self.copy(m).start()

    def take(self, m):
        self.copy(m).wait_recv()
        return decode(self.rcv[self.lead + (m,)])


DIR4 = (1, -1, 1, -1, 1, -1)
DIR8 = (1,) * 7 + (-1,) * 7


def gather_kernel(state_hbm, r_ref, c_hbm, st_ref, gram_ref, cor_ref,
                  rt, sbuf, cbuf, part, cor,
                  sa1, ra1, sa2, ra2, sb1, rb1, sb2, rb2, crecv, cfull, cown,
                  gpart, g1, g2, g3, g4, gown,
                  state_sem, c_sem, ssa1, rsa1, ssa2, rsa2, ssb1, rsb1, ssb2, rsb2,
                  sc, rc, sg1, rg1, sg2, rg2, sg3, rg3, sg4, rg4):
    c, t = lax.axis_index("cell"), lax.axis_index("tm")
    y, z = t // NZ, lax.rem(t, NZ)

    def at_y(o):
        return (c, lax.rem(y + o, NY) * NZ + z)

    def at_z(o):
        return (c, y * NZ + lax.rem(z + o, NZ))

    def at_c(o):
        return (lax.rem(c + o, NC), t)

    barrier = pltpu.get_barrier_semaphore()
    peers = [at_y(o) for o in range(1, NY)] + [at_z(o) for o in range(1, NZ)] + [at_c(o) for o in range(1, NC)]
    for p in peers:
        pl.semaphore_signal(barrier, inc=1, device_id=p, device_id_type=MESH)

    def load(hbm, buf, sem, zo, yo):
        chunk = lax.rem(y + yo, NY) * NZ + lax.rem(z + zo, NZ)
        cols = pl.ds(pl.multiple_of(chunk * OWN, OWN), OWN)
        return pltpu.make_async_copy(hbm.at[:, cols], buf.at[zo, yo], sem.at[zo, yo])

    for zo in ORDER:
        for yo in range(NY):
            load(state_hbm, sbuf, state_sem, zo, yo).start()
    for zo in ORDER:
        for yo in range(NY):
            load(c_hbm, cbuf, c_sem, zo, yo).start()

    rt[...] = (r_ref[...].astype(F32) * SCALE).T.astype(BF16)

    ring_a1 = [Ring((zo,), sa1, ra1, ssa1, rsa1, at_y(1), at_y(NY - 1), DIR4) for zo in range(NZ)]
    ring_a2 = Ring((), sa2, ra2, ssa2, rsa2, at_z(1), at_z(NZ - 1), DIR8)
    ring_b1 = [Ring((yo,), sb1, rb1, ssb1, rsb1, at_z(1), at_z(NZ - 1), DIR8) for yo in range(NY)]
    ring_b2 = Ring((), sb2, rb2, ssb2, rsb2, at_y(1), at_y(NY - 1), DIR4)

    def pa(zo, yo, h):
        return part[zo, yo, 0:A, span(h)]

    def pb(zo, yo, h):
        return part[zo, yo, A:RANK, span(h)]

    def multiply(zo):
        @pl.loop(0, NY)
        def _(yo):
            load(state_hbm, sbuf, state_sem, zo, yo).wait()
            part[zo, yo] = jnp.dot(rt[...], sbuf[zo, yo], preferred_element_type=F32)

    def raw4(ring, own):
        for m, (yo, h) in enumerate(((2, 0), (2, 1), (1, 1), (3, 0))):
            ring.put(m, own(yo, h))
            ring.send(m)

    def acc4(ring, own):
        for m, frm, yo, h in ((4, 0, 1, 0), (5, 1, 3, 1)):
            ring.put(m, own(yo, h) + ring.take(frm))
            ring.send(m)

    def fin4(ring, own):
        return (own(0, 0) + ring.take(3) + ring.take(4), own(0, 1) + ring.take(2) + ring.take(5))

    def far8(ring, own):
        for m, h in ((0, 0), (7, 1)):
            ring.put(m, own(4, h))
            ring.send(m)

    def raw8(ring, own, plus):
        m, zo, h = (4, 3, 1) if plus else (11, 5, 0)
        ring.put(m, own(zo, h))
        ring.send(m)

    def acc8(ring, own, d):
        todo = [(4 - d, d, 0), (11 - d, NZ - d, 1)]
        if d < 3:
            todo += [(7 - d, d, 1), (14 - d, NZ - d, 0)]
        for m, zo, h in todo:
            ring.put(m, own(zo, h) + ring.take(m - 1))
            ring.send(m)

    def fin8(ring, own):
        return (own(0, 0) + ring.take(3) + ring.take(13), own(0, 1) + ring.take(6) + ring.take(10))

    def own_a1(zo):
        return lambda yo, h: pa(zo, yo, h)

    def own_a2(zo, h):
        return pa(zo, 0, h)

    def own_b1(yo):
        return lambda zo, h: pb(zo, yo, h)

    def own_b2(yo, h):
        return pb(0, yo, h)

    def sends(g):
        zo = ORDER[g]
        raw4(ring_a1[zo], own_a1(zo))

    def group(g):
        zo = ORDER[g]
        multiply(zo)
        if zo == 4:
            pl.semaphore_wait(barrier, len(peers))
            for yo in range(NY):
                far8(ring_b1[yo], own_b1(yo))
        if zo in (3, 5):
            for yo in range(NY):
                raw8(ring_b1[yo], own_b1(yo), zo == 3)

    def acc(g):
        zo = ORDER[g]
        acc4(ring_a1[zo], own_a1(zo))

    def y_done(g):
        zo = ORDER[g]
        lo, hi = fin4(ring_a1[zo], own_a1(zo))
        part[zo, 0, 0:A, span(0)] = lo
        part[zo, 0, 0:A, span(1)] = hi
        if zo == 4:
            far8(ring_a2, own_a2)
        if zo in (3, 5):
            raw8(ring_a2, own_a2, zo == 3)

    def b_step(d, yos):
        for yo in yos:
            acc8(ring_b1[yo], own_b1(yo), d)

    def b_done(yos):
        for yo in yos:
            lo, hi = fin8(ring_b1[yo], own_b1(yo))
            part[0, yo, A:RANK, span(0)] = lo
            part[0, yo, A:RANK, span(1)] = hi

    cor[...] = jnp.zeros_like(cor)

    def correlate(gs):
        for g in gs:
            zo = ORDER[g]

            @pl.loop(0, NY)
            def _(yo):
                load(c_hbm, cbuf, c_sem, zo, yo).wait()
                cor[...] += lax.dot_general(
                    cbuf[zo, yo], sbuf[zo, yo], (((1,), (1,)), ((), ())), preferred_element_type=F32
                )

    rows = 256 // NC

    def cor_rs(o):
        at = pl.ds(pl.multiple_of(lax.rem(c + o, NC) * rows, rows), rows)
        return pltpu.make_async_remote_copy(
            cor.at[at], crecv.at[o - 1], sc.at[0, o - 1], rc.at[0, o - 1], device_id=at_c(o), device_id_type=MESH)

    def cor_ag(o):
        return pltpu.make_async_remote_copy(
            cown, cfull.at[o - 1], sc.at[1, o - 1], rc.at[1, o - 1], device_id=at_c(o), device_id_type=MESH)

    mine = pl.ds(pl.multiple_of(c * rows, rows), rows)

    group(0)
    sends(0)
    group(1)
    sends(1)
    group(2)
    sends(2)
    acc(0)
    b_step(3, (0, 1, 2, 3))
    group(3)
    sends(3)
    group(4)
    acc(1)
    y_done(0)
    b_step(2, (0, 1))
    sends(4)
    group(5)
    correlate((0, 1))
    acc(2)
    y_done(1)
    b_step(2, (2, 3))
    sends(5)
    group(6)
    correlate((2, 3))
    acc(3)
    y_done(2)
    acc8(ring_a2, own_a2, 3)
    b_step(1, (0, 1))
    sends(6)
    group(7)
    correlate((4, 5))
    acc(4)
    y_done(3)
    b_step(1, (2, 3))
    sends(7)
    correlate((6, 7))
    for o in range(1, NC):
        cor_rs(o).start()
    acc(5)
    y_done(4)
    acc8(ring_a2, own_a2, 2)
    b_done((0, 1))
    acc(6)
    y_done(5)
    b_done((2, 3))
    raw4(ring_b2, own_b2)
    total = cor[mine]
    for o in range(1, NC):
        cor_rs(o).wait_recv()
        total = total + crecv[o - 1]
    cown[...] = total
    for o in range(1, NC):
        cor_ag(o).start()
    acc(7)
    y_done(6)
    acc8(ring_a2, own_a2, 1)
    acc4(ring_b2, own_b2)
    y_done(7)
    blo, bhi = fin4(ring_b2, own_b2)
    alo, ahi = fin8(ring_a2, own_a2)
    st_ref[A:RANK, span(0)] = blo
    st_ref[A:RANK, span(1)] = bhi
    st_ref[0:A, span(0)] = alo
    st_ref[0:A, span(1)] = ahi

    sk = st_ref[...]
    gpart[...] = lax.dot_general(sk, sk, (((1,), (1,)), ((), ())),
                                 precision=lax.Precision.HIGHEST, preferred_element_type=F32)
    gr = RANK // NC
    mine_g = pl.ds(pl.multiple_of(c * gr, gr), gr)

    def rs1(o):
        at = pl.ds(pl.multiple_of(lax.rem(c + o, NC) * gr, gr), gr)
        return pltpu.make_async_remote_copy(
            gpart.at[at], g1.at[o - 1], sg1.at[o - 1], rg1.at[o - 1], device_id=at_c(o), device_id_type=MESH)

    def ag2(o):
        return pltpu.make_async_remote_copy(
            gown.at[0], g2.at[o - 1], sg2.at[o - 1], rg2.at[o - 1], device_id=at_y(o), device_id_type=MESH)

    def ag3(o):
        return pltpu.make_async_remote_copy(
            gown.at[1], g3.at[o - 1], sg3.at[o - 1], rg3.at[o - 1], device_id=at_z(o), device_id_type=MESH)

    def ag4(o):
        return pltpu.make_async_remote_copy(
            gown.at[2], g4.at[o - 1], sg4.at[o - 1], rg4.at[o - 1], device_id=at_c(o), device_id_type=MESH)

    def phase(make, n, own, recv, slot):
        total = own
        for o in range(1, n):
            make(o).wait_recv()
            total = total + recv[o - 1]
        gown[slot] = total
        return total

    for o in range(1, NC):
        rs1(o).start()
    total = phase(rs1, NC, gpart[mine_g], g1, 0)
    for o in range(1, NY):
        ag2(o).start()
    total = phase(ag2, NY, total, g2, 1)
    for o in range(1, NZ):
        ag3(o).start()
    total = phase(ag3, NZ, total, g3, 2)
    for o in range(1, NC):
        ag4(o).start()
    gram_ref[mine_g] = total

    cor_ref[mine] = cown[...]
    for o in range(1, NC):
        cor_ag(o).wait_recv()
        at = pl.ds(pl.multiple_of(lax.rem(c + NC - o, NC) * rows, rows), rows)
        cor_ref[at] = cfull[o - 1]
    for o in range(1, NC):
        ag4(o).wait_recv()
        at = pl.ds(pl.multiple_of(lax.rem(c + NC - o, NC) * gr, gr), gr)
        gram_ref[at] = g4[o - 1]

    for ring in ring_a1 + [ring_b2]:
        for m in range(6):
            ring.copy(m).wait_send()
    for ring in ring_b1 + [ring_a2]:
        for m in range(14):
            ring.copy(m).wait_send()
    for o in range(1, NC):
        cor_rs(o).wait_send()
        cor_ag(o).wait_send()
        rs1(o).wait_send()
        ag4(o).wait_send()
    for o in range(1, NY):
        ag2(o).wait_send()
    for o in range(1, NZ):
        ag3(o).wait_send()


def gather(state, range_test, corange_test):
    dma = pltpu.SemaphoreType.DMA
    B = RANK - A

    def bf(*s):
        return pltpu.VMEM(s, BF16)

    def fl(*s):
        return pltpu.VMEM(s, F32)

    vmem = pl.BlockSpec(memory_space=pltpu.VMEM)
    hbm = pl.BlockSpec(memory_space=pl.ANY)
    return pl.pallas_call(
        gather_kernel,
        name="sketch_sums",
        out_shape=(
            jax.ShapeDtypeStruct((RANK, OWN), F32),
            jax.ShapeDtypeStruct((RANK, RANK), F32),
            jax.ShapeDtypeStruct((256, 256), F32),
        ),
        in_specs=[hbm, vmem, hbm],
        out_specs=(vmem, vmem, vmem),
        scratch_shapes=[
            bf(RANK, STEPS), bf(NZ, NY, STEPS, OWN), bf(NZ, NY, 256, OWN), fl(NZ, NY, RANK, OWN), fl(256, 256),
            bf(NZ, 6, A, HALF), bf(NZ, 6, A, HALF), bf(14, A, HALF), bf(14, A, HALF),
            bf(NY, 14, B, HALF), bf(NY, 14, B, HALF), bf(6, B, HALF), bf(6, B, HALF),
            fl(7, 32, 256), fl(7, 32, 256), fl(32, 256),
            fl(RANK, RANK), fl(7, 16, RANK), fl(3, 16, RANK), fl(7, 16, RANK), fl(7, 16, RANK), fl(3, 16, RANK),
            dma((NZ, NY)), dma((NZ, NY)),
            dma((NZ, 6)), dma((NZ, 6)), dma((14,)), dma((14,)),
            dma((NY, 14)), dma((NY, 14)), dma((6,)), dma((6,)),
            dma((2, 7)), dma((2, 7)),
            dma((7,)), dma((7,)), dma((3,)), dma((3,)), dma((7,)), dma((7,)), dma((7,)), dma((7,)),
        ],
        compiler_params=pltpu.CompilerParams(
            collective_id=1, has_side_effects=True, vmem_limit_bytes=56 << 20),
    )(state, range_test, corange_test)


def factor_kernel(scale, gram_ref, st_ref, out_ref, w_ref):
    n = RANK
    lane = lax.broadcasted_iota(jnp.int32, (1, n), 1)
    sub = lax.broadcasted_iota(jnp.int32, (n, 1), 0)
    w = gram_ref[...]
    for k in range(n - 1):
        top = (k + 1) // 8 * 8
        low = w[top:]
        row = w[k:k + 1]
        pivot = w[k:k + 1, k:k + 1]
        col = low[:, k:k + 1]
        mult = jnp.where(sub[top:] > k, col / pivot, 0.0)
        hit = (lane == k) & (sub[top:] > k)
        row = jnp.where(lane == k, 1.0, row)
        low = jnp.where(hit, 0.0, low) - mult * row
        w = jnp.concatenate([w[:top], low], axis=0) if top else low
    diag = jnp.sum(jnp.where(lane == sub, w, 0.0), axis=1, keepdims=True)
    unit = jnp.where(lane < sub, w, jnp.where(lane == sub, 1.0, 0.0))
    w_ref[...] = unit * (scale * lax.rsqrt(diag))
    out_ref[...] = lax.dot_general(st_ref[...], w_ref[...], (((0,), (1,)), ((), ())),
                                   precision=lax.Precision.HIGHEST, preferred_element_type=F32)


def factor(gram, st, scale):
    vmem = pl.BlockSpec(memory_space=pltpu.VMEM)
    return pl.pallas_call(
        functools.partial(factor_kernel, scale),
        name="factor",
        out_shape=jax.ShapeDtypeStruct((OWN, RANK), F32),
        in_specs=[vmem, vmem],
        out_specs=vmem,
        scratch_shapes=[pltpu.VMEM((RANK, RANK), F32)],
        compiler_params=pltpu.CompilerParams(vmem_limit_bytes=32 << 20),
    )(gram, st)


def on_device(state, range_test, corange_test):
    total_cells = state.shape[1] * NC
    st, gram, corange = gather(state, range_test, corange_test)
    basis = factor(gram, st, float(total_cells) ** 0.5)
    return (basis, corange)


def solution(mesh):
    return jax.shard_map(
        on_device,
        mesh=mesh,
        in_specs=(P("tm", "cell"), P("tm", None), P(None, "cell")),
        out_specs=(P(("cell", "tm"), None), P(None, "tm")),
        check_vma=False,
    )
```

time: 547 us -> 81.2 us (0.15)
  waiting for transfers between devices: 482 us -> 0 us
  Pallas kernels: 0 us -> 76.9 us
  other arithmetic: 23.7 us -> 0 us
  matrix products: 22.1 us -> 0 us
  between operations: 13.8 us -> 0.65 us
    psum x3 -> x0, waiting for transfers between devices: 482 us -> none  [the longest x1 231 us: on_device(): gram = lax.psum(gram_part, ('cell', 'tm'))]
    pallas_call x0 -> x2, Pallas kernels: none -> 76.9 us  [the longest x1 65.2 us: gather(): pl.pallas_call(gather_kernel, name='sketch_sums', out_shape=(jax.ShapeDty...]
    another operation x5 -> x0, other arithmetic: 22.9 us -> none  [the longest x3 12.4 us: on_device(): lower = jnp.linalg.cholesky(gram)]
    dot_general x3 -> x0, matrix products: 20.1 us -> none  [the longest x1 9 us: on_device(): lax.dot_general(state, range_test, (((0,), (0,)), ((), ())), preferred_el...]
  transfers between devices with their start and end apart: 3 -> 0, of which waited for: 3 -> 0; matrix products, arithmetic and copies ran while one was open for 7% -> 0% of each run, Pallas kernels for 0% -> 0%
where the time goes in v1:
time: 81.2 us; the launch traced here: 81 us
  Pallas kernels  76.9 us (95%)
  local copies, waits for them, and re-layouts  3.45 us (4%)
    pallas_call x1, Pallas kernels, gather(): pl.pallas_call(gather_kernel, name='sketch_sums', out_shape=(jax.ShapeDty...  65.2 us
    pallas_call x1, Pallas kernels, factor(): pl.pallas_call(functools.partial(factor_kernel, scale), name='factor', ou...  11.7 us
    unnamed x5, local copies, waits for them, and re-layouts  3.45 us

profile of v1, /device:TPU:1, one launch (start us, length us, event | category | flops | bytes accessed | tf_op | source)
XLA Modules:
  0.0 81.0 jit_solution(14541959660545068578)
XLA Ops:
  0.6 65.2 %sketch_sums.1 = (f32[128,512]{1,0:T(8,128)}, f32[128,128]{1,0:T(8,128)}, f32[256,256]{1,0:T(8,128)}) custom-call(bf16[256,16384]{1,0:T(8,128)(2,1)} %state_hbm.1, bf16[256,128]{1,0:T(8,128)(2,1)} %r_ref.1, bf16[256,16384]{1,0:T(8,128)(2,1)} %c_hbm.1), custom_call_target="tpu_custom_call" | custom-call | tf_op jit(solution)/shard_map/sketch_sums/pallas_call | solution.py:375
  65.8 0.0 copy-start
  65.8 0.9 %copy-done = f32[128,512]{1,0:T(8,128)S(1)} copy-done((f32[128,512]{1,0:T(8,128)S(1)}, f32[128,512]{1,0:T(8,128)}, u32[]{:S(2)}) %copy-start) | copy-done | bytes 262168
  66.8 0.0 copy-start.1
  66.8 0.8 %copy-done.1 = f32[128,128]{1,0:T(8,128)S(1)} copy-done((f32[128,128]{1,0:T(8,128)S(1)}, f32[128,128]{1,0:T(8,128)}, u32[]{:S(2)}) %copy-start.1) | copy-done | bytes 65560
  67.6 11.7 %factor.1 = f32[512,128]{1,0:T(8,128)} custom-call(f32[128,128]{1,0:T(8,128)S(1)} %copy-done.1, f32[128,512]{1,0:T(8,128)S(1)} %copy-done), custom_call_target="tpu_custom_call" | custom-call | tf_op jit(solution)/shard_map/factor/pallas_call | solution.py:427
  79.3 1.7 %copy.6 = f32[256,256]{1,0:T(8,128)} copy(f32[256,256]{1,0:T(8,128)} %get-tuple-element.11) | data formatting | bytes 524288
Async XLA Ops:
  65.8 1.0 %copy-start = (f32[128,512]{1,0:T(8,128)S(1)}, f32[128,512]{1,0:T(8,128)}, u32[]{:S(2)}) copy-start(f32[128,512]{1,0:T(8,128)} %get-tuple-element.6.st_ref) | copy-start | bytes 786436
  66.8 0.8 %copy-start.1 = (f32[128,128]{1,0:T(8,128)S(1)}, f32[128,128]{1,0:T(8,128)}, u32[]{:S(2)}) copy-start(f32[128,128]{1,0:T(8,128)} %get-tuple-element.5.gram_ref) | copy-start | bytes 196612

commit v2 on v1

v2 whole, which is shorter than its diff:
```python
import functools

import jax
import jax.numpy as jnp
from jax import lax
from jax.experimental import pallas as pl
from jax.experimental.pallas import tpu as pltpu
from jax.sharding import PartitionSpec as P

MESH = pl.DeviceIdType.MESH
F32, BF16 = jnp.float32, jnp.bfloat16
NY, NZ, NC = 4, 8, 8
RANK, STEPS, OWN, HALF = 128, 256, 512, 256
A = 80
SCALE = 32768.0
ORDER = (4, 3, 5, 2, 6, 1, 7, 0)
FAR_C = (4, 5, 3, 2, 6, 7, 1)

SCHEDULE = (
    ("g", 0), ("s", 0), ("g", 1), ("g", 2), ("s", 1), ("g", 3), ("c", 2), ("b3", 1), ("c", 1), ("s", 2),
    ("a", 0), ("s", 3), ("g", 4), ("b3", 0), ("b3", 3), ("c", 4), ("g", 5), ("g", 6), ("b3", 2), ("b2", 1),
    ("g", 7), ("a", 1), ("s", 4), ("b2", 0), ("b2", 2), ("c", 6), ("b2", 3), ("a", 2), ("y", 0), ("c", 0),
    ("c", 5), ("c", 7), ("c", 3), ("cs",), ("y", 1), ("a", 3), ("b1", 2), ("b1", 0), ("s", 5), ("y", 2),
    ("A3",), ("b1", 3), ("s", 6), ("a", 4), ("b1", 1), ("y", 3), ("a", 5), ("b0", 0), ("cq",), ("a", 6),
    ("s", 7), ("b0", 2), ("b0", 3), ("y", 4), ("A2",), ("b0", 1), ("y", 5), ("r",), ("y", 6), ("a", 7),
    ("A1",), ("q",), ("y", 7),
)


def encode(x):
    s = x * x
    return (s * x * jnp.abs(x)).astype(BF16)


def decode(y):
    y = y.astype(F32)
    r = lax.rsqrt(lax.rsqrt(jnp.maximum(jnp.abs(y), 1.2e-38)))
    return jnp.where(y < 0, -r, r)


def span(h):
    return pl.ds(h * HALF, HALF)


class Ring:
    def __init__(self, lead, snd, rcv, ssem, rsem, plus, minus, targets):
        self.lead, self.snd, self.rcv = lead, snd, rcv
        self.ssem, self.rsem = ssem, rsem
        self.ids = {1: plus, -1: minus}
        self.targets = targets

    def copy(self, m):
        i = self.lead + (m,)
        return pltpu.make_async_remote_copy(
            self.snd.at[i], self.rcv.at[i], self.ssem.at[i], self.rsem.at[i],
            device_id=self.ids[self.targets[m]], device_id_type=MESH,
        )

    def put(self, m, value):
        self.snd[self.lead + (m,)] = encode(value)

    def send(self, m):
        self.copy(m).start()

    def take(self, m):
        self.copy(m).wait_recv()
        return decode(self.rcv[self.lead + (m,)])


DIR4 = (1, -1, 1, -1, 1, -1)
DIR8 = (1,) * 7 + (-1,) * 7


def gather_kernel(state_hbm, r_ref, c_hbm, st_out, gram_out, cor_out,
                  rt, sbuf, cbuf, part, cor,
                  sa1, ra1, sa2, ra2, sb1, rb1, sb2, rb2, crecv, cfull,
                  st, gpart, g1, g2, g3, g4,
                  state_sem, c_sem, ssa1, rsa1, ssa2, rsa2, ssb1, rsb1, ssb2, rsb2,
                  sc, rc, sg1, rg1, sg2, rg2, sg3, rg3, sg4, rg4, out_sem):
    c, t = lax.axis_index("cell"), lax.axis_index("tm")
    y, z = t // NZ, lax.rem(t, NZ)

    def at_y(o):
        return (c, lax.rem(y + o, NY) * NZ + z)

    def at_z(o):
        return (c, y * NZ + lax.rem(z + o, NZ))

    def at_c(o):
        return (lax.rem(c + o, NC), t)

    barrier = pltpu.get_barrier_semaphore()
    peers = [at_y(o) for o in range(1, NY)] + [at_z(o) for o in range(1, NZ)] + [at_c(o) for o in range(1, NC)]
    for p in peers:
        pl.semaphore_signal(barrier, inc=1, device_id=p, device_id_type=MESH)

    def load(hbm, buf, sem, zo, yo):
        chunk = lax.rem(y + yo, NY) * NZ + lax.rem(z + zo, NZ)
        cols = pl.ds(pl.multiple_of(chunk * OWN, OWN), OWN)
        return pltpu.make_async_copy(hbm.at[:, cols], buf.at[zo, yo], sem.at[zo, yo])

    for zo in ORDER:
        for yo in range(NY):
            load(state_hbm, sbuf, state_sem, zo, yo).start()
    for zo in ORDER:
        for yo in range(NY):
            load(c_hbm, cbuf, c_sem, zo, yo).start()

    rt[...] = (r_ref[...].astype(F32) * SCALE).T.astype(BF16)

    ring_a1 = [Ring((zo,), sa1, ra1, ssa1, rsa1, at_y(1), at_y(NY - 1), DIR4) for zo in range(NZ)]
    ring_a2 = Ring((), sa2, ra2, ssa2, rsa2, at_z(1), at_z(NZ - 1), DIR8)
    ring_b1 = [Ring((yo,), sb1, rb1, ssb1, rsb1, at_z(1), at_z(NZ - 1), DIR8) for yo in range(NY)]
    ring_b2 = Ring((), sb2, rb2, ssb2, rsb2, at_y(1), at_y(NY - 1), DIR4)

    def pa(zo, yo, h):
        return part[zo, yo, 0:A, span(h)]

    def pb(zo, yo, h):
        return part[zo, yo, A:RANK, span(h)]

    def multiply(zo):
        @pl.loop(0, NY)
        def _(yo):
            load(state_hbm, sbuf, state_sem, zo, yo).wait()
            part[zo, yo] = jnp.dot(rt[...], sbuf[zo, yo], preferred_element_type=F32)

    def raw4(ring, own):
        for m, (yo, h) in enumerate(((2, 0), (2, 1), (1, 1), (3, 0))):
            ring.put(m, own(yo, h))
            ring.send(m)

    def acc4(ring, own):
        for m, frm, yo, h in ((4, 0, 1, 0), (5, 1, 3, 1)):
            ring.put(m, own(yo, h) + ring.take(frm))
            ring.send(m)

    def fin4(ring, own):
        return (own(0, 0) + ring.take(3) + ring.take(4), own(0, 1) + ring.take(2) + ring.take(5))

    def far8(ring, own):
        for m, h in ((0, 0), (7, 1)):
            ring.put(m, own(4, h))
            ring.send(m)

    def raw8(ring, own, plus):
        m, zo, h = (4, 3, 1) if plus else (11, 5, 0)
        ring.put(m, own(zo, h))
        ring.send(m)

    def acc8(ring, own, d):
        todo = [(4 - d, d, 0), (11 - d, NZ - d, 1)]
        if d < 3:
            todo += [(7 - d, d, 1), (14 - d, NZ - d, 0)]
        for m, zo, h in todo:
            ring.put(m, own(zo, h) + ring.take(m - 1))
            ring.send(m)

    def fin8(ring, own):
        return (own(0, 0) + ring.take(3) + ring.take(13), own(0, 1) + ring.take(6) + ring.take(10))

    def own_a1(zo):
        return lambda yo, h: pa(zo, yo, h)

    def own_a2(zo, h):
        return pa(zo, 0, h)

    def own_b1(yo):
        return lambda zo, h: pb(zo, yo, h)

    def own_b2(yo, h):
        return pb(0, yo, h)

    def sends(g):
        zo = ORDER[g]
        raw4(ring_a1[zo], own_a1(zo))

    def group(g):
        zo = ORDER[g]
        multiply(zo)
        if zo == 4:
            pl.semaphore_wait(barrier, len(peers))
            for yo in range(NY):
                far8(ring_b1[yo], own_b1(yo))
        if zo in (3, 5):
            for yo in range(NY):
                raw8(ring_b1[yo], own_b1(yo), zo == 3)

    def acc(g):
        zo = ORDER[g]
        acc4(ring_a1[zo], own_a1(zo))

    def y_done(g):
        zo = ORDER[g]
        lo, hi = fin4(ring_a1[zo], own_a1(zo))
        part[zo, 0, 0:A, span(0)] = lo
        part[zo, 0, 0:A, span(1)] = hi
        if zo == 4:
            far8(ring_a2, own_a2)
        if zo in (3, 5):
            raw8(ring_a2, own_a2, zo == 3)

    def b_step(d):
        return lambda yo: acc8(ring_b1[yo], own_b1(yo), d)

    def b_done(yo):
        lo, hi = fin8(ring_b1[yo], own_b1(yo))
        part[0, yo, A:RANK, span(0)] = lo
        part[0, yo, A:RANK, span(1)] = hi

    cor[...] = jnp.zeros_like(cor)

    def correlate(g):
        zo = ORDER[g]

        @pl.loop(0, NY)
        def _(yo):
            load(c_hbm, cbuf, c_sem, zo, yo).wait()
            cor[...] += lax.dot_general(
                cbuf[zo, yo], sbuf[zo, yo], (((1,), (1,)), ((), ())), preferred_element_type=F32
            )

    rows = 256 // NC

    def strip(i, n):
        return pl.ds(pl.multiple_of(i * n, n), n)

    def near_c(o):
        return lax.rem(c + o, NC)

    def cor_rs(o):
        return pltpu.make_async_remote_copy(
            cor.at[strip(near_c(o), rows)], crecv.at[o - 1], sc.at[0, o - 1], rc.at[0, o - 1],
            device_id=at_c(o), device_id_type=MESH)

    def cor_ag(o, owner):
        return pltpu.make_async_remote_copy(
            cfull.at[strip(owner, rows)], cfull.at[strip(owner, rows)], sc.at[1, o - 1], rc.at[1, owner],
            device_id=at_c(o), device_id_type=MESH)

    def cor_send():
        for o in FAR_C:
            cor_rs(o).start()

    def cor_sum():
        total = cor[strip(c, rows)]
        for o in range(1, NC):
            cor_rs(o).wait_recv()
            total = total + crecv[o - 1]
        cfull[strip(c, rows)] = total
        for o in FAR_C:
            cor_ag(o, c).start()

    acts = {
        "g": group, "s": sends, "a": acc, "y": y_done, "c": correlate, "cs": cor_send, "cq": cor_sum,
        "b3": b_step(3), "b2": b_step(2), "b1": b_step(1), "b0": b_done,
        "A3": lambda: acc8(ring_a2, own_a2, 3),
        "A2": lambda: acc8(ring_a2, own_a2, 2),
        "A1": lambda: acc8(ring_a2, own_a2, 1),
        "r": lambda: raw4(ring_b2, own_b2),
        "q": lambda: acc4(ring_b2, own_b2),
    }
    for act, *which in SCHEDULE:
        acts[act](*which)

    blo, bhi = fin4(ring_b2, own_b2)
    st[A:RANK, span(0)] = blo
    st[A:RANK, span(1)] = bhi
    alo, ahi = fin8(ring_a2, own_a2)
    st[0:A, span(0)] = alo
    st[0:A, span(1)] = ahi

    sk = st[...]
    gpart[...] = lax.dot_general(sk, sk, (((1,), (1,)), ((), ())),
                                 precision=lax.Precision.HIGHEST, preferred_element_type=F32)
    gr = RANK // NC

    def rs1(o):
        return pltpu.make_async_remote_copy(
            gpart.at[strip(near_c(o), gr)], g1.at[o - 1], sg1.at[o - 1], rg1.at[o - 1],
            device_id=at_c(o), device_id_type=MESH)

    def ag2(o, owner):
        return pltpu.make_async_remote_copy(
            g2.at[owner], g2.at[owner], sg2.at[o - 1], rg2.at[owner], device_id=at_y(o), device_id_type=MESH)

    def ag3(o, owner):
        return pltpu.make_async_remote_copy(
            g3.at[owner], g3.at[owner], sg3.at[o - 1], rg3.at[owner], device_id=at_z(o), device_id_type=MESH)

    def ag4(o, owner):
        return pltpu.make_async_remote_copy(
            g4.at[strip(owner, gr)], g4.at[strip(owner, gr)], sg4.at[o - 1], rg4.at[owner],
            device_id=at_c(o), device_id_type=MESH)

    for o in FAR_C:
        rs1(o).start()
    outs = [pltpu.make_async_copy(st, st_out, out_sem.at[0]),
            pltpu.make_async_copy(cfull, cor_out, out_sem.at[1]),
            pltpu.make_async_copy(g4, gram_out, out_sem.at[2])]
    outs[0].start()
    total = gpart[strip(c, gr)]
    for o in FAR_C[::-1]:
        rs1(o).wait_recv()
        total = total + g1[o - 1]
    g2[y] = total
    for o in (2, 1, 3):
        ag2(o, y).start()
    for o in range(1, NC):
        cor_ag(o, near_c(o)).wait_recv()
    outs[1].start()
    for o in (1, 3, 2):
        ag2(o, lax.rem(y + o, NY)).wait_recv()
    total = g2[0]
    for i in range(1, NY):
        total = total + g2[i]
    g3[z] = total
    for o in (4, 3, 5, 2, 6, 1, 7):
        ag3(o, z).start()
    for ring in ring_a1 + [ring_b2]:
        for m in range(6):
            ring.copy(m).wait_send()
    for ring in ring_b1 + [ring_a2]:
        for m in range(14):
            ring.copy(m).wait_send()
    for o in range(1, NC):
        cor_rs(o).wait_send()
        cor_ag(o, c).wait_send()
        rs1(o).wait_send()
    for o in range(1, NY):
        ag2(o, y).wait_send()
    for o in (1, 7, 2, 6, 3, 5, 4):
        ag3(o, lax.rem(z + o, NZ)).wait_recv()
    total = g3[0]
    for i in range(1, NZ):
        total = total + g3[i]
    g4[strip(c, gr)] = total
    for o in FAR_C:
        ag4(o, c).start()
    for o in range(1, NZ):
        ag3(o, z).wait_send()
    outs[0].wait()
    outs[1].wait()
    for o in FAR_C[::-1]:
        ag4(o, near_c(o)).wait_recv()
    outs[2].start()
    for o in range(1, NC):
        ag4(o, c).wait_send()
    outs[2].wait()


def gather(state, range_test, corange_test):
    dma = pltpu.SemaphoreType.DMA
    B = RANK - A

    def bf(*s):
        return pltpu.VMEM(s, BF16)

    def fl(*s):
        return pltpu.VMEM(s, F32)

    vmem = pl.BlockSpec(memory_space=pltpu.VMEM)
    hbm = pl.BlockSpec(memory_space=pl.ANY)
    return pl.pallas_call(
        gather_kernel,
        name="sketch_sums",
        out_shape=(
            jax.ShapeDtypeStruct((RANK, OWN), F32),
            jax.ShapeDtypeStruct((RANK, RANK), F32),
            jax.ShapeDtypeStruct((256, 256), F32),
        ),
        in_specs=[hbm, vmem, hbm],
        out_specs=(hbm, hbm, hbm),
        scratch_shapes=[
            bf(RANK, STEPS), bf(NZ, NY, STEPS, OWN), bf(NZ, NY, 256, OWN), fl(NZ, NY, RANK, OWN), fl(256, 256),
            bf(NZ, 6, A, HALF), bf(NZ, 6, A, HALF), bf(14, A, HALF), bf(14, A, HALF),
            bf(NY, 14, B, HALF), bf(NY, 14, B, HALF), bf(6, B, HALF), bf(6, B, HALF),
            fl(7, 32, 256), fl(256, 256),
            fl(RANK, OWN), fl(RANK, RANK), fl(7, 16, RANK), fl(NY, 16, RANK), fl(NZ, 16, RANK), fl(RANK, RANK),
            dma((NZ, NY)), dma((NZ, NY)),
            dma((NZ, 6)), dma((NZ, 6)), dma((14,)), dma((14,)),
            dma((NY, 14)), dma((NY, 14)), dma((6,)), dma((6,)),
            dma((2, 7)), dma((2, NC)),
            dma((7,)), dma((7,)), dma((3,)), dma((NY,)), dma((7,)), dma((NZ,)), dma((7,)), dma((NC,)), dma((3,)),
        ],
        compiler_params=pltpu.CompilerParams(
            collective_id=1, has_side_effects=True, vmem_limit_bytes=56 << 20),
    )(state, range_test, corange_test)


def inverse_factor(w, scale):
    lane = lax.broadcasted_iota(jnp.int32, (8, RANK), 1)
    sub = lax.broadcasted_iota(jnp.int32, (8, RANK), 0)
    full = (8, RANK)
    out = []
    for b in range(RANK // 8):
        k = 8 * b
        inside = (lane >= k) & (lane < k + 8)
        cols = [jnp.broadcast_to(w[b][:, k + j:k + j + 1], full) for j in range(8)]
        p = [[jnp.broadcast_to(cols[j][i:i + 1], full) for j in range(i + 1)] for i in range(8)]
        l = [[None] * 8 for _ in range(8)]
        inv = []
        for j in range(8):
            inv.append(1.0 / p[j][j])
            for i in range(j + 1, 8):
                l[i][j] = p[i][j] * inv[j]
            for i in range(j + 1, 8):
                for m in range(j + 1, i + 1):
                    p[i][m] = p[i][m] - l[i][j] * p[m][j]
        own = jnp.where(inside, jnp.where(lane - k == sub, 1.0, 0.0), w[b])
        rows = []
        for i in range(8):
            r = jnp.broadcast_to(own[i:i + 1], full)
            for j in range(i):
                r = r - l[i][j] * rows[j]
            rows.append(r)
        done = jnp.zeros(full, F32)
        for i in range(8):
            done = jnp.where(sub == i, rows[i] * (scale * lax.rsqrt(p[i][i])), done)
        out.append(jnp.where(lane < k + 8, done, 0.0))
        for rb in range(b + 1, RANK // 8):
            q = []
            new = jnp.where(inside, 0.0, w[rb])
            for j in range(8):
                v = jnp.broadcast_to(w[rb][:, k + j:k + j + 1], full)
                for i in range(j):
                    v = v - q[i] * l[j][i]
                q.append(v)
            for j in range(8):
                new = new - (q[j] * inv[j]) * rows[j]
            w[rb] = new
    return jnp.concatenate(out, axis=0)


def factor_kernel(scale, gram_hbm, st_hbm, cor_hbm, out_ref, cor_out, gram, st, w_ref, sem):
    loads = [pltpu.make_async_copy(gram_hbm, gram, sem.at[0]),
             pltpu.make_async_copy(st_hbm, st, sem.at[1]),
             pltpu.make_async_copy(cor_hbm, cor_out, sem.at[2])]
    for copy in loads:
        copy.start()
    loads[0].wait()
    w = [gram[8 * b:8 * b + 8] for b in range(RANK // 8)]
    w_ref[...] = inverse_factor(w, scale)
    loads[1].wait()
    out_ref[...] = lax.dot_general(st[...], w_ref[...], (((0,), (1,)), ((), ())),
                                   precision=lax.Precision.HIGHEST, preferred_element_type=F32)
    loads[2].wait()


def factor(gram, st, cor, scale):
    hbm = pl.BlockSpec(memory_space=pl.ANY)
    return pl.pallas_call(
        functools.partial(factor_kernel, scale),
        name="factor",
        out_shape=(jax.ShapeDtypeStruct((OWN, RANK), F32), jax.ShapeDtypeStruct(cor.shape, F32)),
        in_specs=[hbm, hbm, hbm],
        out_specs=(pl.BlockSpec(memory_space=pltpu.VMEM), hbm),
        scratch_shapes=[pltpu.VMEM((RANK, RANK), F32), pltpu.VMEM((RANK, OWN), F32), pltpu.VMEM((RANK, RANK), F32),
                        pltpu.SemaphoreType.DMA((3,))],
        compiler_params=pltpu.CompilerParams(vmem_limit_bytes=56 << 20),
    )(gram, st, cor)


def on_device(state, range_test, corange_test):
    total_cells = state.shape[1] * NC
    st, gram, corange = gather(state, range_test, corange_test)
    return factor(gram, st, corange, float(total_cells) ** 0.5)


def solution(mesh):
    return jax.shard_map(
        on_device,
        mesh=mesh,
        in_specs=(P("tm", "cell"), P("tm", None), P(None, "cell")),
        out_specs=(P(("cell", "tm"), None), P(None, "tm")),
        check_vma=False,
    )
```

time: 81.2 us -> 75.8 us (0.933)
  local copies, waits for them, and re-layouts: 3.45 us -> 0 us
  Pallas kernels: 76.9 us -> 74.8 us
    unnamed x5 -> x0, local copies, waits for them, and re-layouts: 3.45 us -> none
    pallas_call x1, Pallas kernels: 11.7 us -> 9.77 us  [factor(): pl.pallas_call(functools.partial(factor_kernel, scale), name='factor', ou...]
where the time goes in v2:
time: 75.8 us; the launch traced here: 75.6 us
  Pallas kernels  74.8 us (99%)
  between operations  0.8 us (1%)
    pallas_call x1, Pallas kernels, gather(): pl.pallas_call(gather_kernel, name='sketch_sums', out_shape=(jax.ShapeDty...  65.1 us
    pallas_call x1, Pallas kernels, factor(): pl.pallas_call(functools.partial(factor_kernel, scale), name='factor', ou...  9.77 us

profile of v2, /device:TPU:1, one launch (start us, length us, event | category | flops | bytes accessed | tf_op | source)
XLA Modules:
  0.0 75.6 jit_solution(11552674117068155099)
XLA Ops:
  0.6 65.1 %sketch_sums.1 = (f32[128,512]{1,0:T(8,128)}, f32[128,128]{1,0:T(8,128)}, f32[256,256]{1,0:T(8,128)}) custom-call(bf16[256,16384]{1,0:T(8,128)(2,1)} %state_hbm.1, bf16[256,128]{1,0:T(8,128)(2,1)} %r_ref.1, bf16[256,16384]{1,0:T(8,128)(2,1)} %c_hbm.1), custom_call_target="tpu_custom_call" | custom-call | tf_op jit(solution)/shard_map/sketch_sums/pallas_call | solution.py:364
  65.7 9.8 %factor.1 = (f32[512,128]{1,0:T(8,128)}, f32[256,256]{1,0:T(8,128)}) custom-call(f32[128,128]{1,0:T(8,128)} %get-tuple-element.5.gram_hbm, f32[128,512]{1,0:T(8,128)} %get-tuple-element.6.st_hbm, f32[256,256]{1,0:T(8,128)} %get-tuple-element.7.cor_hbm), custom_call_target="tpu_custom_call" | custom-call | tf_op jit(solution)/shard_map/factor/pallas_call | solution.py:452

commit v3 on v2

v3 whole, which is shorter than its diff:
```python
import functools

import jax
import jax.numpy as jnp
from jax import lax
from jax.experimental import pallas as pl
from jax.experimental.pallas import tpu as pltpu
from jax.sharding import PartitionSpec as P

MESH = pl.DeviceIdType.MESH
F32, BF16 = jnp.float32, jnp.bfloat16
NY, NZ, NC = 4, 8, 8
RANK, STEPS, OWN, HALF = 128, 256, 512, 256
A = 80
SCALE = 32768.0
ORDER = (4, 3, 5, 2, 6, 1, 7, 0)
FAR_C = (4, 5, 3, 2, 6, 7, 1)

GROUPS = ((0, 1), (1, 2), (3, 2), (5, 2), (7, 1))
PLUS, MINUS = 0, 1
SCHEDULE = (
    ("g", 0), ("s", 0), ("g", 1), ("g", 2), ("s", 1), ("c", 0), ("g", 3), ("c", 1), ("c", 2), ("b3", 0),
    ("a", 0), ("g", 4), ("s", 2), ("b2", 1), ("c", 3), ("g", 5), ("a", 1), ("b2", 0), ("c", 4), ("y", 0),
    ("g", 6), ("b1", 1), ("c", 5), ("s", 3), ("c", 6), ("a", 2), ("g", 7), ("b1", 0), ("c", 7), ("cs",),
    ("y", 1), ("A3",), ("s", 4), ("a", 3), ("b0",), ("y", 2), ("A2",), ("cq",), ("r",), ("a", 4), ("y", 3),
    ("A1",), ("q",), ("y", 4),
)


def encode(x):
    s = x * x
    return (s * x * jnp.abs(x)).astype(BF16)


def decode(y):
    y = y.astype(F32)
    r = lax.rsqrt(lax.rsqrt(jnp.maximum(jnp.abs(y), 1.2e-38)))
    return jnp.where(y < 0, -r, r)


def span(h):
    return pl.ds(h * HALF, HALF)


def gather_kernel(state_hbm, r_ref, c_hbm, st_out, gram_out, cor_out,
                  rt, sbuf, cbuf, part, cor,
                  sraw, rraw, sacc, racc, sz, rz, sb, rb, sraw2, rraw2, sacc2, racc2, crecv, cfull,
                  st, gpart, g1, g2, g3, g4,
                  load_sem, sem_raw, sem_acc, sem_z, sem_b, sem_raw2, sem_acc2,
                  sc, rc, sg1, rg1, sg2, rg2, sg3, rg3, sg4, rg4, out_sem):
    c, t = lax.axis_index("cell"), lax.axis_index("tm")
    y, z = t // NZ, lax.rem(t, NZ)

    def at_y(o):
        return (c, lax.rem(y + o, NY) * NZ + z)

    def at_z(o):
        return (c, y * NZ + lax.rem(z + o, NZ))

    def at_c(o):
        return (lax.rem(c + o, NC), t)

    barrier = pltpu.get_barrier_semaphore()
    peers = [at_y(o) for o in range(1, NY)] + [at_z(o) for o in range(1, NZ)] + [at_c(o) for o in range(1, NC)]
    for p in peers:
        pl.semaphore_signal(barrier, inc=1, device_id=p, device_id_type=MESH)

    def load(hbm, buf, i, yo):
        cols = pl.ds(pl.multiple_of(lax.rem(y + yo, NY) * (NZ * OWN), NZ * OWN), NZ * OWN)
        return pltpu.make_async_copy(hbm.at[:, cols], buf.at[yo], load_sem.at[i, yo])

    for yo in range(NY):
        load(state_hbm, sbuf, 0, yo).start()
    for yo in range(NY):
        load(c_hbm, cbuf, 1, yo).start()

    rt[...] = (r_ref[...].astype(F32) * SCALE).T.astype(BF16)

    to_y = (at_y(1), at_y(NY - 1))
    to_z = (at_z(1), at_z(NZ - 1))
    pending = []

    def message(src, dst, sems, i, to):
        return pltpu.make_async_remote_copy(
            src, dst, sems.at[(0,) + i], sems.at[(1,) + i], device_id=to, device_id_type=MESH)

    def send(copy):
        copy.start()
        pending.append(copy)

    def lanes(zo):
        return pl.ds(pl.multiple_of(lax.rem(z + zo, NZ) * OWN, OWN), OWN)

    def multiply(p):
        zo = ORDER[p]

        @pl.loop(0, NY)
        def _(yo):
            part[zo, yo] = jnp.dot(rt[...], sbuf[yo, :, lanes(zo)], preferred_element_type=F32)

    def pa(zo, yo, h):
        return part[zo, yo, 0:A, span(h)]

    def pb(zo, yo, h):
        return part[zo, yo, A:RANK, span(h)]

    def raw_y(d, put, own):
        put(0, encode(own(2, d)))
        put(1, encode(own(1 if d == PLUS else 3, 1 - d)))

    def a_raw(g, d):
        at = pl.ds(*GROUPS[g])
        return message(sraw.at[d, at], rraw.at[d, at], sem_raw, (d, g), to_y[d])

    def a_acc(g, d):
        at = pl.ds(*GROUPS[g])
        return message(sacc.at[d, at], racc.at[d, at], sem_acc, (d, g), to_y[d])

    def positions(g):
        return range(GROUPS[g][0], GROUPS[g][0] + GROUPS[g][1])

    def sends(g):
        for d in (PLUS, MINUS):
            for p in positions(g):
                def put(slot, value):
                    sraw[d, p, slot] = value

                raw_y(d, put, lambda yo, h: pa(ORDER[p], yo, h))
            send(a_raw(g, d))

    def acc(g):
        for d in (PLUS, MINUS):
            a_raw(g, d).wait_recv()
            for p in positions(g):
                own = pa(ORDER[p], 1 if d == PLUS else 3, d)
                sacc[d, p] = encode(own + decode(rraw[d, p, 0]))
            send(a_acc(g, d))

    def z_msg(d, k):
        src, dst = (sz.at[d, 0, 0], rz.at[d, 0, 0]) if k == 4 else (sz.at[d, 4 - k], rz.at[d, 4 - k])
        return message(src, dst, sem_z, (d, 4 - k), to_z[d])

    def toward(d, k):
        return k if d == PLUS else NZ - k

    def z_far():
        for d in (PLUS, MINUS):
            sz[d, 0, 0] = encode(pa(4, 0, d))
            send(z_msg(d, 4))

    def z_step(k):
        for d in (PLUS, MINUS):
            zo = toward(d, k)
            z_msg(d, k + 1).wait_recv()
            sz[d, 4 - k, 0] = encode(pa(zo, 0, d) + decode(rz[d, 3 - k, 0]))
            other = pa(zo, 0, 1 - d)
            sz[d, 4 - k, 1] = encode(other if k == 3 else other + decode(rz[d, 3 - k, 1]))
            send(z_msg(d, k))

    def y_done(g):
        for d in (PLUS, MINUS):
            a_acc(g, d).wait_recv()
        for p in positions(g):
            zo = ORDER[p]
            for h in (0, 1):
                part[zo, 0, 0:A, span(h)] = pa(zo, 0, h) + decode(rraw[1 - h, p, 1]) + decode(racc[h, p])
        if g == 0:
            z_far()

    def b_msg(d, k, chain):
        i = (d, 4 - k, chain)
        return message(sb.at[i], rb.at[i], sem_b, i, to_z[d])

    def b_raw(d, k, chain):
        for yo in range(NY):
            sb[d, 4 - k, chain, yo] = encode(pb(toward(d, k), yo, d if chain == 0 else 1 - d))
        send(b_msg(d, k, chain))

    def b_step(k):
        def go(chain):
            for d in (PLUS, MINUS):
                b_msg(d, k + 1, chain).wait_recv()
                for yo in range(NY):
                    own = pb(toward(d, k), yo, d if chain == 0 else 1 - d)
                    sb[d, 4 - k, chain, yo] = encode(own + decode(rb[d, 3 - k, chain, yo]))
                send(b_msg(d, k, chain))

        return go

    def b_done():
        for d in (PLUS, MINUS):
            for chain in (0, 1):
                b_msg(d, 1, chain).wait_recv()
        for yo in range(NY):
            for h in (0, 1):
                part[0, yo, A:RANK, span(h)] = (
                    pb(0, yo, h) + decode(rb[h, 3, 0, yo]) + decode(rb[1 - h, 3, 1, yo]))

    def r_msg(d):
        return message(sraw2.at[d], rraw2.at[d], sem_raw2, (d,), to_y[d])

    def q_msg(d):
        return message(sacc2.at[d], racc2.at[d], sem_acc2, (d,), to_y[d])

    def raw2():
        for d in (PLUS, MINUS):
            def put(slot, value):
                sraw2[d, slot] = value

            raw_y(d, put, lambda yo, h: pb(0, yo, h))
            send(r_msg(d))

    def acc2():
        for d in (PLUS, MINUS):
            r_msg(d).wait_recv()
            sacc2[d] = encode(pb(0, 1 if d == PLUS else 3, d) + decode(rraw2[d, 0]))
            send(q_msg(d))

    def group(p):
        if p == 0:
            for yo in range(NY):
                load(state_hbm, sbuf, 0, yo).wait()
        multiply(p)
        if p == 0:
            pl.semaphore_wait(barrier, len(peers))
            b_raw(PLUS, 4, 0)
            b_raw(MINUS, 4, 0)
        if p in (1, 2):
            b_raw(p - 1, 3, 1)

    cor[...] = jnp.zeros_like(cor)

    def correlate(p):
        zo = ORDER[p]
        if p == 0:
            for yo in range(NY):
                load(c_hbm, cbuf, 1, yo).wait()

        @pl.loop(0, NY)
        def _(yo):
            cor[...] += lax.dot_general(
                cbuf[yo, :, lanes(zo)], sbuf[yo, :, lanes(zo)], (((1,), (1,)), ((), ())), preferred_element_type=F32
            )

    rows = 256 // NC

    def strip(i, n):
        return pl.ds(pl.multiple_of(i * n, n), n)

    def near_c(o):
        return lax.rem(c + o, NC)

    def cor_rs(o):
        return pltpu.make_async_remote_copy(
            cor.at[strip(near_c(o), rows)], crecv.at[o - 1], sc.at[0, o - 1], rc.at[0, o - 1],
            device_id=at_c(o), device_id_type=MESH)

    def cor_ag(o, owner):
        return pltpu.make_async_remote_copy(
            cfull.at[strip(owner, rows)], cfull.at[strip(owner, rows)], sc.at[1, o - 1], rc.at[1, owner],
            device_id=at_c(o), device_id_type=MESH)

    def cor_send():
        for o in FAR_C:
            cor_rs(o).start()

    def cor_sum():
        total = cor[strip(c, rows)]
        for o in range(1, NC):
            cor_rs(o).wait_recv()
            total = total + crecv[o - 1]
        cfull[strip(c, rows)] = total
        for o in FAR_C:
            cor_ag(o, c).start()

    acts = {
        "g": group, "s": sends, "a": acc, "y": y_done, "c": correlate, "cs": cor_send, "cq": cor_sum,
        "b3": b_step(3), "b2": b_step(2), "b1": b_step(1), "b0": b_done,
        "A3": lambda: z_step(3), "A2": lambda: z_step(2), "A1": lambda: z_step(1), "r": raw2, "q": acc2,
    }
    for act, *which in SCHEDULE:
        acts[act](*which)

    for d in (PLUS, MINUS):
        q_msg(d).wait_recv()
    for h in (0, 1):
        st[A:RANK, span(h)] = pb(0, 0, h) + decode(rraw2[1 - h, 1]) + decode(racc2[h])
    for d in (PLUS, MINUS):
        z_msg(d, 1).wait_recv()
    for h in (0, 1):
        st[0:A, span(h)] = pa(0, 0, h) + decode(rz[h, 3, 0]) + decode(rz[1 - h, 3, 1])

    sk = st[...]
    gpart[...] = lax.dot_general(sk, sk, (((1,), (1,)), ((), ())),
                                 precision=lax.Precision.HIGHEST, preferred_element_type=F32)
    gr = RANK // NC

    def rs1(o):
        return pltpu.make_async_remote_copy(
            gpart.at[strip(near_c(o), gr)], g1.at[o - 1], sg1.at[o - 1], rg1.at[o - 1],
            device_id=at_c(o), device_id_type=MESH)

    def ag2(o, owner):
        return pltpu.make_async_remote_copy(
            g2.at[owner], g2.at[owner], sg2.at[o - 1], rg2.at[owner], device_id=at_y(o), device_id_type=MESH)

    def ag3(o, owner):
        return pltpu.make_async_remote_copy(
            g3.at[owner], g3.at[owner], sg3.at[o - 1], rg3.at[owner], device_id=at_z(o), device_id_type=MESH)

    def ag4(o, owner):
        return pltpu.make_async_remote_copy(
            g4.at[strip(owner, gr)], g4.at[strip(owner, gr)], sg4.at[o - 1], rg4.at[owner],
            device_id=at_c(o), device_id_type=MESH)

    for o in FAR_C:
        rs1(o).start()
    outs = [pltpu.make_async_copy(st, st_out, out_sem.at[0]),
            pltpu.make_async_copy(cfull, cor_out, out_sem.at[1]),
            pltpu.make_async_copy(g4, gram_out, out_sem.at[2])]
    outs[0].start()
    total = gpart[strip(c, gr)]
    for o in FAR_C[::-1]:
        rs1(o).wait_recv()
        total = total + g1[o - 1]
    g2[y] = total
    for o in (2, 1, 3):
        ag2(o, y).start()
    for o in range(1, NC):
        cor_ag(o, near_c(o)).wait_recv()
    outs[1].start()
    for o in (1, 3, 2):
        ag2(o, lax.rem(y + o, NY)).wait_recv()
    total = g2[0]
    for i in range(1, NY):
        total = total + g2[i]
    g3[z] = total
    for o in (4, 3, 5, 2, 6, 1, 7):
        ag3(o, z).start()
    for copy in pending:
        copy.wait_send()
    for o in range(1, NC):
        cor_rs(o).wait_send()
        cor_ag(o, c).wait_send()
        rs1(o).wait_send()
    for o in range(1, NY):
        ag2(o, y).wait_send()
    for o in (1, 7, 2, 6, 3, 5, 4):
        ag3(o, lax.rem(z + o, NZ)).wait_recv()
    total = g3[0]
    for i in range(1, NZ):
        total = total + g3[i]
    g4[strip(c, gr)] = total
    for o in FAR_C:
        ag4(o, c).start()
    for o in range(1, NZ):
        ag3(o, z).wait_send()
    outs[0].wait()
    outs[1].wait()
    for o in FAR_C[::-1]:
        ag4(o, near_c(o)).wait_recv()
    outs[2].start()
    for o in range(1, NC):
        ag4(o, c).wait_send()
    outs[2].wait()


def gather(state, range_test, corange_test):
    dma = pltpu.SemaphoreType.DMA
    B = RANK - A

    def bf(*s):
        return pltpu.VMEM(s, BF16)

    def fl(*s):
        return pltpu.VMEM(s, F32)

    vmem = pl.BlockSpec(memory_space=pltpu.VMEM)
    hbm = pl.BlockSpec(memory_space=pl.ANY)
    return pl.pallas_call(
        gather_kernel,
        name="sketch_sums",
        out_shape=(
            jax.ShapeDtypeStruct((RANK, OWN), F32),
            jax.ShapeDtypeStruct((RANK, RANK), F32),
            jax.ShapeDtypeStruct((256, 256), F32),
        ),
        in_specs=[hbm, vmem, hbm],
        out_specs=(hbm, hbm, hbm),
        scratch_shapes=[
            bf(RANK, STEPS), bf(NY, STEPS, NZ * OWN), bf(NY, 256, NZ * OWN), fl(NZ, NY, RANK, OWN), fl(256, 256),
            bf(2, NZ, 2, A, HALF), bf(2, NZ, 2, A, HALF), bf(2, NZ, A, HALF), bf(2, NZ, A, HALF),
            bf(2, 4, 2, A, HALF), bf(2, 4, 2, A, HALF), bf(2, 4, 2, NY, B, HALF), bf(2, 4, 2, NY, B, HALF),
            bf(2, 2, B, HALF), bf(2, 2, B, HALF), bf(2, B, HALF), bf(2, B, HALF),
            fl(7, 32, 256), fl(256, 256),
            fl(RANK, OWN), fl(RANK, RANK), fl(7, 16, RANK), fl(NY, 16, RANK), fl(NZ, 16, RANK), fl(RANK, RANK),
            dma((2, NY)), dma((2, 2, 5)), dma((2, 2, 5)), dma((2, 2, 4)), dma((2, 2, 4, 2)), dma((2, 2)), dma((2, 2)),
            dma((2, 7)), dma((2, NC)),
            dma((7,)), dma((7,)), dma((3,)), dma((NY,)), dma((7,)), dma((NZ,)), dma((7,)), dma((NC,)), dma((3,)),
        ],
        compiler_params=pltpu.CompilerParams(
            collective_id=1, has_side_effects=True, vmem_limit_bytes=56 << 20),
    )(state, range_test, corange_test)


def inverse_factor(w, scale, midway):
    lane = lax.broadcasted_iota(jnp.int32, (8, RANK), 1)
    sub = lax.broadcasted_iota(jnp.int32, (8, RANK), 0)
    full = (8, RANK)
    out = []
    for b in range(RANK // 8):
        k = 8 * b
        if b == 6:
            midway()
        inside = (lane >= k) & (lane < k + 8)
        cols = [jnp.broadcast_to(w[b][:, k + j:k + j + 1], full) for j in range(8)]
        p = [[jnp.broadcast_to(cols[j][i:i + 1], full) for j in range(i + 1)] for i in range(8)]
        l = [[None] * 8 for _ in range(8)]
        inv = []
        for j in range(8):
            inv.append(1.0 / p[j][j])
            for i in range(j + 1, 8):
                l[i][j] = p[i][j] * inv[j]
            for i in range(j + 1, 8):
                for m in range(j + 1, i + 1):
                    p[i][m] = p[i][m] - l[i][j] * p[m][j]
        own = jnp.where(inside, jnp.where(lane - k == sub, 1.0, 0.0), w[b])
        rows = []
        for i in range(8):
            r = jnp.broadcast_to(own[i:i + 1], full)
            for j in range(i):
                r = r - l[i][j] * rows[j]
            rows.append(r)
        done = jnp.zeros(full, F32)
        for i in range(8):
            done = jnp.where(sub == i, rows[i] * (scale * lax.rsqrt(p[i][i])), done)
        out.append(jnp.where(lane < k + 8, done, 0.0))
        for rb in range(b + 1, RANK // 8):
            q = []
            new = jnp.where(inside, 0.0, w[rb])
            for j in range(8):
                v = jnp.broadcast_to(w[rb][:, k + j:k + j + 1], full)
                for i in range(j):
                    v = v - q[i] * l[j][i]
                q.append(v)
            for j in range(8):
                new = new - (q[j] * inv[j]) * rows[j]
            w[rb] = new
    return jnp.concatenate(out, axis=0)


def factor_kernel(scale, gram_hbm, st_hbm, cor_hbm, out_ref, cor_out, gram, st, cor, w_ref, sem):
    loads = [pltpu.make_async_copy(gram_hbm, gram, sem.at[0]),
             pltpu.make_async_copy(cor_hbm, cor, sem.at[1]),
             pltpu.make_async_copy(st_hbm, st, sem.at[2])]
    for copy in loads:
        copy.start()
    store = pltpu.make_async_copy(cor, cor_out, sem.at[3])

    def midway():
        loads[1].wait()
        store.start()

    loads[0].wait()
    w = [gram[8 * b:8 * b + 8] for b in range(RANK // 8)]
    w_ref[...] = inverse_factor(w, scale, midway)
    loads[2].wait()
    out_ref[...] = lax.dot_general(st[...], w_ref[...], (((0,), (1,)), ((), ())),
                                   precision=lax.Precision.HIGHEST, preferred_element_type=F32)
    store.wait()


def factor(gram, st, cor, scale):
    hbm = pl.BlockSpec(memory_space=pl.ANY)
    return pl.pallas_call(
        functools.partial(factor_kernel, scale),
        name="factor",
        out_shape=(jax.ShapeDtypeStruct((OWN, RANK), F32), jax.ShapeDtypeStruct(cor.shape, F32)),
        in_specs=[hbm, hbm, hbm],
        out_specs=(pl.BlockSpec(memory_space=pltpu.VMEM), hbm),
        scratch_shapes=[pltpu.VMEM((RANK, RANK), F32), pltpu.VMEM((RANK, OWN), F32), pltpu.VMEM(cor.shape, F32),
                        pltpu.VMEM((RANK, RANK), F32), pltpu.SemaphoreType.DMA((4,))],
        compiler_params=pltpu.CompilerParams(vmem_limit_bytes=56 << 20),
    )(gram, st, cor)


def on_device(state, range_test, corange_test):
    total_cells = state.shape[1] * NC
    st, gram, corange = gather(state, range_test, corange_test)
    return factor(gram, st, corange, float(total_cells) ** 0.5)


def solution(mesh):
    return jax.shard_map(
        on_device,
        mesh=mesh,
        in_specs=(P("tm", "cell"), P("tm", None), P(None, "cell")),
        out_specs=(P(("cell", "tm"), None), P(None, "tm")),
        check_vma=False,
    )
```

time: 75.8 us -> 68.3 us (0.901)
  Pallas kernels: 74.8 us -> 67.5 us
    pallas_call x1, Pallas kernels: 9.77 us -> 5.95 us  [factor(): pl.pallas_call(functools.partial(factor_kernel, scale), name='factor', ou...]
    pallas_call x1, Pallas kernels: 65.1 us -> 61.6 us  [gather(): pl.pallas_call(gather_kernel, name='sketch_sums', out_shape=(jax.ShapeDty...]
where the time goes in v3:
time: 68.3 us; the launch traced here: 68.2 us
  Pallas kernels  67.5 us (99%)
    pallas_call x1, Pallas kernels, gather(): pl.pallas_call(gather_kernel, name='sketch_sums', out_shape=(jax.ShapeDty...  61.6 us
    pallas_call x1, Pallas kernels, factor(): pl.pallas_call(functools.partial(factor_kernel, scale), name='factor', ou...  5.95 us

profile of v3, /device:TPU:1, one launch (start us, length us, event | category | flops | bytes accessed | tf_op | source)
XLA Modules:
  0.0 68.2 jit_solution(3943667524607987731)
XLA Ops:
  0.6 61.6 %sketch_sums.1 = (f32[128,512]{1,0:T(8,128)}, f32[128,128]{1,0:T(8,128)}, f32[256,256]{1,0:T(8,128)}) custom-call(bf16[256,16384]{1,0:T(8,128)(2,1)} %state_hbm.1, bf16[256,128]{1,0:T(8,128)(2,1)} %r_ref.1, bf16[256,16384]{1,0:T(8,128)(2,1)} %c_hbm.1), custom_call_target="tpu_custom_call" | custom-call | tf_op jit(solution)/shard_map/sketch_sums/pallas_call | solution.py:380
  62.2 6.0 %factor.1 = (f32[512,128]{1,0:T(8,128)}, f32[256,256]{1,0:T(8,128)}) custom-call(f32[128,128]{1,0:T(8,128)} %get-tuple-element.5.gram_hbm, f32[128,512]{1,0:T(8,128)} %get-tuple-element.6.st_hbm, f32[256,256]{1,0:T(8,128)} %get-tuple-element.7.cor_hbm), custom_call_target="tpu_custom_call" | custom-call | tf_op jit(solution)/shard_map/factor/pallas_call | solution.py:475

commit v4 on v3

--- a/solution.py
+++ b/solution.py
@@ -19,10 +19,10 @@
 GROUPS = ((0, 1), (1, 2), (3, 2), (5, 2), (7, 1))
 PLUS, MINUS = 0, 1
 SCHEDULE = (
-    ("g", 0), ("s", 0), ("g", 1), ("g", 2), ("s", 1), ("c", 0), ("g", 3), ("c", 1), ("c", 2), ("b3", 0),
-    ("a", 0), ("g", 4), ("s", 2), ("b2", 1), ("c", 3), ("g", 5), ("a", 1), ("b2", 0), ("c", 4), ("y", 0),
-    ("g", 6), ("b1", 1), ("c", 5), ("s", 3), ("c", 6), ("a", 2), ("g", 7), ("b1", 0), ("c", 7), ("cs",),
-    ("y", 1), ("A3",), ("s", 4), ("a", 3), ("b0",), ("y", 2), ("A2",), ("cq",), ("r",), ("a", 4), ("y", 3),
+    ("g", 0), ("s", 0), ("g", 1), ("g", 2), ("s", 1), ("g", 3), ("c", 0), ("g", 4), ("c", 1), ("b3", 0),
+    ("a", 0), ("s", 2), ("g", 5), ("g", 6), ("c", 2), ("b2", 1), ("a", 1), ("c", 3), ("c", 4), ("y", 0),
+    ("g", 7), ("b2", 0), ("c", 5), ("s", 3), ("c", 6), ("b1", 1), ("c", 7), ("cs",), ("y", 1), ("A3",),
+    ("a", 2), ("b1", 0), ("s", 4), ("a", 3), ("y", 2), ("A2",), ("cq",), ("b0",), ("r",), ("a", 4), ("y", 3),
     ("A1",), ("q",), ("y", 4),
 )
 
@@ -42,8 +42,8 @@
     return pl.ds(h * HALF, HALF)
 
 
-def gather_kernel(state_hbm, r_ref, c_hbm, st_out, gram_out, cor_out,
-                  rt, sbuf, cbuf, part, cor,
+def gather_kernel(state_hbm, r_hbm, c_hbm, st_out, gram_out, cor_out,
+                  rbuf, rt, sbuf, cbuf, part, cor,
                   sraw, rraw, sacc, racc, sz, rz, sb, rb, sraw2, rraw2, sacc2, racc2, crecv, cfull,
                   st, gpart, g1, g2, g3, g4,
                   load_sem, sem_raw, sem_acc, sem_z, sem_b, sem_raw2, sem_acc2,
@@ -69,12 +69,15 @@
         cols = pl.ds(pl.multiple_of(lax.rem(y + yo, NY) * (NZ * OWN), NZ * OWN), NZ * OWN)
         return pltpu.make_async_copy(hbm.at[:, cols], buf.at[yo], load_sem.at[i, yo])
 
+    load_r = pltpu.make_async_copy(r_hbm, rbuf, out_sem.at[3])
+    load_r.start()
     for yo in range(NY):
         load(state_hbm, sbuf, 0, yo).start()
     for yo in range(NY):
         load(c_hbm, cbuf, 1, yo).start()
 
-    rt[...] = (r_ref[...].astype(F32) * SCALE).T.astype(BF16)
+    load_r.wait()
+    rt[...] = (rbuf[...].astype(F32) * SCALE).T.astype(BF16)
 
     to_y = (at_y(1), at_y(NY - 1))
     to_z = (at_z(1), at_z(NZ - 1))
@@ -228,19 +231,16 @@
         if p in (1, 2):
             b_raw(p - 1, 3, 1)
 
-    cor[...] = jnp.zeros_like(cor)
-
-    def correlate(p):
-        zo = ORDER[p]
-        if p == 0:
+    wide = NZ * OWN // 2
+
+    def correlate(i):
+        if i == 0:
             for yo in range(NY):
                 load(c_hbm, cbuf, 1, yo).wait()
-
-        @pl.loop(0, NY)
-        def _(yo):
-            cor[...] += lax.dot_general(
-                cbuf[yo, :, lanes(zo)], sbuf[yo, :, lanes(zo)], (((1,), (1,)), ((), ())), preferred_element_type=F32
-            )
+        cols = pl.ds(i % 2 * wide, wide)
+        product = lax.dot_general(
+            cbuf[i // 2, :, cols], sbuf[i // 2, :, cols], (((1,), (1,)), ((), ())), preferred_element_type=F32)
+        cor[...] = product if i == 0 else cor[...] + product
 
     rows = 256 // NC
 
@@ -291,6 +291,7 @@
         st[0:A, span(h)] = pa(0, 0, h) + decode(rz[h, 3, 0]) + decode(rz[1 - h, 3, 1])
 
     sk = st[...]
+    st_out[...] = sk
     gpart[...] = lax.dot_general(sk, sk, (((1,), (1,)), ((), ())),
                                  precision=lax.Precision.HIGHEST, preferred_element_type=F32)
     gr = RANK // NC
@@ -315,10 +316,6 @@
 
     for o in FAR_C:
         rs1(o).start()
-    outs = [pltpu.make_async_copy(st, st_out, out_sem.at[0]),
-            pltpu.make_async_copy(cfull, cor_out, out_sem.at[1]),
-            pltpu.make_async_copy(g4, gram_out, out_sem.at[2])]
-    outs[0].start()
     total = gpart[strip(c, gr)]
     for o in FAR_C[::-1]:
         rs1(o).wait_recv()
@@ -328,7 +325,7 @@
         ag2(o, y).start()
     for o in range(1, NC):
         cor_ag(o, near_c(o)).wait_recv()
-    outs[1].start()
+    cor_out[...] = cfull[...]
     for o in (1, 3, 2):
         ag2(o, lax.rem(y + o, NY)).wait_recv()
     total = g2[0]
@@ -355,14 +352,11 @@
         ag4(o, c).start()
     for o in range(1, NZ):
         ag3(o, z).wait_send()
-    outs[0].wait()
-    outs[1].wait()
     for o in FAR_C[::-1]:
         ag4(o, near_c(o)).wait_recv()
-    outs[2].start()
+    gram_out[...] = g4[...]
     for o in range(1, NC):
         ag4(o, c).wait_send()
-    outs[2].wait()
 
 
 def gather(state, range_test, corange_test):
@@ -380,15 +374,11 @@
     return pl.pallas_call(
         gather_kernel,
         name="sketch_sums",
-        out_shape=(
-            jax.ShapeDtypeStruct((RANK, OWN), F32),
-            jax.ShapeDtypeStruct((RANK, RANK), F32),
-            jax.ShapeDtypeStruct((256, 256), F32),
-        ),
-        in_specs=[hbm, vmem, hbm],
-        out_specs=(hbm, hbm, hbm),
+        out_shape=(pltpu.VMEM((RANK, OWN), F32), pltpu.VMEM((RANK, RANK), F32), pltpu.VMEM((256, 256), F32)),
+        in_specs=[hbm, hbm, hbm],
+        out_specs=(vmem, vmem, vmem),
         scratch_shapes=[
-            bf(RANK, STEPS), bf(NY, STEPS, NZ * OWN), bf(NY, 256, NZ * OWN), fl(NZ, NY, RANK, OWN), fl(256, 256),
+            bf(STEPS, RANK), bf(RANK, STEPS), bf(NY, STEPS, NZ * OWN), bf(NY, 256, NZ * OWN), fl(NZ, NY, RANK, OWN), fl(256, 256),
             bf(2, NZ, 2, A, HALF), bf(2, NZ, 2, A, HALF), bf(2, NZ, A, HALF), bf(2, NZ, A, HALF),
             bf(2, 4, 2, A, HALF), bf(2, 4, 2, A, HALF), bf(2, 4, 2, NY, B, HALF), bf(2, 4, 2, NY, B, HALF),
             bf(2, 2, B, HALF), bf(2, 2, B, HALF), bf(2, B, HALF), bf(2, B, HALF),
@@ -396,22 +386,20 @@
             fl(RANK, OWN), fl(RANK, RANK), fl(7, 16, RANK), fl(NY, 16, RANK), fl(NZ, 16, RANK), fl(RANK, RANK),
             dma((2, NY)), dma((2, 2, 5)), dma((2, 2, 5)), dma((2, 2, 4)), dma((2, 2, 4, 2)), dma((2, 2)), dma((2, 2)),
             dma((2, 7)), dma((2, NC)),
-            dma((7,)), dma((7,)), dma((3,)), dma((NY,)), dma((7,)), dma((NZ,)), dma((7,)), dma((NC,)), dma((3,)),
+            dma((7,)), dma((7,)), dma((3,)), dma((NY,)), dma((7,)), dma((NZ,)), dma((7,)), dma((NC,)), dma((4,)),
         ],
         compiler_params=pltpu.CompilerParams(
-            collective_id=1, has_side_effects=True, vmem_limit_bytes=56 << 20),
+            collective_id=1, has_side_effects=True, vmem_limit_bytes=60 << 20),
     )(state, range_test, corange_test)
 
 
-def inverse_factor(w, scale, midway):
+def inverse_factor(w, scale):
     lane = lax.broadcasted_iota(jnp.int32, (8, RANK), 1)
     sub = lax.broadcasted_iota(jnp.int32, (8, RANK), 0)
     full = (8, RANK)
     out = []
     for b in range(RANK // 8):
         k = 8 * b
-        if b == 6:
-            midway()
         inside = (lane >= k) & (lane < k + 8)
         cols = [jnp.broadcast_to(w[b][:, k + j:k + j + 1], full) for j in range(8)]
         p = [[jnp.broadcast_to(cols[j][i:i + 1], full) for j in range(i + 1)] for i in range(8)]
@@ -449,38 +437,30 @@
     return jnp.concatenate(out, axis=0)
 
 
-def factor_kernel(scale, gram_hbm, st_hbm, cor_hbm, out_ref, cor_out, gram, st, cor, w_ref, sem):
-    loads = [pltpu.make_async_copy(gram_hbm, gram, sem.at[0]),
-             pltpu.make_async_copy(cor_hbm, cor, sem.at[1]),
-             pltpu.make_async_copy(st_hbm, st, sem.at[2])]
-    for copy in loads:
-        copy.start()
-    store = pltpu.make_async_copy(cor, cor_out, sem.at[3])
-
-    def midway():
-        loads[1].wait()
-        store.start()
-
-    loads[0].wait()
+def factor_kernel(scale, gram, st, cor, out_hbm, cor_out, basis, w_ref, sem):
+    store = pltpu.make_async_copy(cor, cor_out, sem.at[0])
+    store.start()
     w = [gram[8 * b:8 * b + 8] for b in range(RANK // 8)]
-    w_ref[...] = inverse_factor(w, scale, midway)
-    loads[2].wait()
-    out_ref[...] = lax.dot_general(st[...], w_ref[...], (((0,), (1,)), ((), ())),
-                                   precision=lax.Precision.HIGHEST, preferred_element_type=F32)
+    w_ref[...] = inverse_factor(w, scale)
+    basis[...] = lax.dot_general(st[...], w_ref[...], (((0,), (1,)), ((), ())),
+                                 precision=lax.Precision.HIGHEST, preferred_element_type=F32)
+    out = pltpu.make_async_copy(basis, out_hbm, sem.at[1])
+    out.start()
     store.wait()
+    out.wait()
 
 
 def factor(gram, st, cor, scale):
     hbm = pl.BlockSpec(memory_space=pl.ANY)
+    vmem = pl.BlockSpec(memory_space=pltpu.VMEM)
     return pl.pallas_call(
         functools.partial(factor_kernel, scale),
         name="factor",
         out_shape=(jax.ShapeDtypeStruct((OWN, RANK), F32), jax.ShapeDtypeStruct(cor.shape, F32)),
-        in_specs=[hbm, hbm, hbm],
-        out_specs=(pl.BlockSpec(memory_space=pltpu.VMEM), hbm),
-        scratch_shapes=[pltpu.VMEM((RANK, RANK), F32), pltpu.VMEM((RANK, OWN), F32), pltpu.VMEM(cor.shape, F32),
-                        pltpu.VMEM((RANK, RANK), F32), pltpu.SemaphoreType.DMA((4,))],
-        compiler_params=pltpu.CompilerParams(vmem_limit_bytes=56 << 20),
+        in_specs=[vmem, vmem, vmem],
+        out_specs=(hbm, hbm),
+        scratch_shapes=[pltpu.VMEM((OWN, RANK), F32), pltpu.VMEM((RANK, RANK), F32), pltpu.SemaphoreType.DMA((2,))],
+        compiler_params=pltpu.CompilerParams(vmem_limit_bytes=32 << 20),
     )(gram, st, cor)
 
 

time: 68.3 us -> 66.4 us (0.972)
  Pallas kernels: 67.5 us -> 65.7 us
    pallas_call x1, Pallas kernels: 61.6 us -> 60.2 us  [gather(): pl.pallas_call(gather_kernel, name='sketch_sums', out_shape=(pltpu.VMEM((...]
where the time goes in v4:
time: 66.4 us; the launch traced here: 66.3 us
  Pallas kernels  65.7 us (99%)
    pallas_call x1, Pallas kernels, gather(): pl.pallas_call(gather_kernel, name='sketch_sums', out_shape=(pltpu.VMEM((...  60.2 us
    pallas_call x1, Pallas kernels, factor(): pl.pallas_call(functools.partial(factor_kernel, scale), name='factor', ou...  5.43 us

profile of v4, /device:TPU:1, one launch (start us, length us, event | category | flops | bytes accessed | tf_op | source)
XLA Modules:
  0.0 66.3 jit_solution(16930314154373438641)
XLA Ops:
  0.6 60.2 %sketch_sums.1 = (f32[128,512]{1,0:T(8,128)S(1)}, f32[128,128]{1,0:T(8,128)S(1)}, f32[256,256]{1,0:T(8,128)S(1)}) custom-call(bf16[256,16384]{1,0:T(8,128)(2,1)} %state_hbm.1, bf16[256,128]{1,0:T(8,128)(2,1)} %r_hbm.1, bf16[256,16384]{1,0:T(8,128)(2,1)} %c_hbm.1), custom_call_target="tpu_custom_call" | custom-call | tf_op jit(solution)/shard_map/sketch_sums/pallas_call | solution.py:374
  60.9 5.4 %factor.1 = (f32[512,128]{1,0:T(8,128)}, f32[256,256]{1,0:T(8,128)}) custom-call(f32[128,128]{1,0:T(8,128)S(1)} %get-tuple-element.5.gram, f32[128,512]{1,0:T(8,128)S(1)} %get-tuple-element.6.st, f32[256,256]{1,0:T(8,128)S(1)} %get-tuple-element.7.cor), custom_call_target="tpu_custom_call" | custom-call | tf_op jit(solution)/shard_map/factor/pallas_call | solution.py:456

commit v5 on v4

--- a/solution.py
+++ b/solution.py
@@ -19,10 +19,10 @@
 GROUPS = ((0, 1), (1, 2), (3, 2), (5, 2), (7, 1))
 PLUS, MINUS = 0, 1
 SCHEDULE = (
-    ("g", 0), ("s", 0), ("g", 1), ("g", 2), ("s", 1), ("g", 3), ("c", 0), ("g", 4), ("c", 1), ("b3", 0),
-    ("a", 0), ("s", 2), ("g", 5), ("g", 6), ("c", 2), ("b2", 1), ("a", 1), ("c", 3), ("c", 4), ("y", 0),
-    ("g", 7), ("b2", 0), ("c", 5), ("s", 3), ("c", 6), ("b1", 1), ("c", 7), ("cs",), ("y", 1), ("A3",),
-    ("a", 2), ("b1", 0), ("s", 4), ("a", 3), ("y", 2), ("A2",), ("cq",), ("b0",), ("r",), ("a", 4), ("y", 3),
+    ("g", 0), ("s", 0), ("g", 1), ("g", 2), ("s", 1), ("c", 0), ("g", 3), ("a", 0), ("b3", 0), ("g", 4),
+    ("c", 1), ("g", 5), ("s", 2), ("b2", 1), ("g", 6), ("a", 1), ("g", 7), ("b2", 0), ("c", 2), ("y", 0),
+    ("c", 3), ("b1", 1), ("s", 3), ("c", 4), ("c", 5), ("c", 6), ("a", 2), ("y", 1), ("A3",), ("c", 7),
+    ("cs",), ("b1", 0), ("s", 4), ("a", 3), ("y", 2), ("A2",), ("b0",), ("r",), ("cq",), ("a", 4), ("y", 3),
     ("A1",), ("q",), ("y", 4),
 )
 
@@ -43,9 +43,9 @@
 
 
 def gather_kernel(state_hbm, r_hbm, c_hbm, st_out, gram_out, cor_out,
-                  rbuf, rt, sbuf, cbuf, part, cor,
+                  rbuf, rt, sfirst, sbuf, cbuf, part, cor,
                   sraw, rraw, sacc, racc, sz, rz, sb, rb, sraw2, rraw2, sacc2, racc2, crecv, cfull,
-                  st, gpart, g1, g2, g3, g4,
+                  gpart, g1, g2, g3, g4,
                   load_sem, sem_raw, sem_acc, sem_z, sem_b, sem_raw2, sem_acc2,
                   sc, rc, sg1, rg1, sg2, rg2, sg3, rg3, sg4, rg4, out_sem):
     c, t = lax.axis_index("cell"), lax.axis_index("tm")
@@ -61,7 +61,7 @@
         return (lax.rem(c + o, NC), t)
 
     barrier = pltpu.get_barrier_semaphore()
-    peers = [at_y(o) for o in range(1, NY)] + [at_z(o) for o in range(1, NZ)] + [at_c(o) for o in range(1, NC)]
+    peers = [at_y(1), at_y(NY - 1), at_z(1), at_z(NZ - 1)] + [at_c(o) for o in range(1, NC)]
     for p in peers:
         pl.semaphore_signal(barrier, inc=1, device_id=p, device_id_type=MESH)
 
@@ -71,6 +71,14 @@
 
     load_r = pltpu.make_async_copy(r_hbm, rbuf, out_sem.at[3])
     load_r.start()
+
+    def load_first(yo):
+        chunk = lax.rem(y + yo, NY) * NZ + lax.rem(z + ORDER[0], NZ)
+        cols = pl.ds(pl.multiple_of(chunk * OWN, OWN), OWN)
+        return pltpu.make_async_copy(state_hbm.at[:, cols], sfirst.at[yo], load_sem.at[2, yo])
+
+    for yo in range(NY):
+        load_first(yo).start()
     for yo in range(NY):
         load(state_hbm, sbuf, 0, yo).start()
     for yo in range(NY):
@@ -99,7 +107,8 @@
 
         @pl.loop(0, NY)
         def _(yo):
-            part[zo, yo] = jnp.dot(rt[...], sbuf[yo, :, lanes(zo)], preferred_element_type=F32)
+            block = sfirst[yo] if p == 0 else sbuf[yo, :, lanes(zo)]
+            part[zo, yo] = jnp.dot(rt[...], block, preferred_element_type=F32)
 
     def pa(zo, yo, h):
         return part[zo, yo, 0:A, span(h)]
@@ -139,9 +148,11 @@
                 sacc[d, p] = encode(own + decode(rraw[d, p, 0]))
             send(a_acc(g, d))
 
-    def z_msg(d, k):
-        src, dst = (sz.at[d, 0, 0], rz.at[d, 0, 0]) if k == 4 else (sz.at[d, 4 - k], rz.at[d, 4 - k])
-        return message(src, dst, sem_z, (d, 4 - k), to_z[d])
+    def z_msg(d, k, chain=0):
+        i = (d, 4 - k)
+        if k in (2, 3):
+            return message(sz.at[i], rz.at[i], sem_z, i + (0,), to_z[d])
+        return message(sz.at[i + (chain,)], rz.at[i + (chain,)], sem_z, i + (chain,), to_z[d])
 
     def toward(d, k):
         return k if d == PLUS else NZ - k
@@ -153,12 +164,16 @@
 
     def z_step(k):
         for d in (PLUS, MINUS):
-            zo = toward(d, k)
             z_msg(d, k + 1).wait_recv()
-            sz[d, 4 - k, 0] = encode(pa(zo, 0, d) + decode(rz[d, 3 - k, 0]))
-            other = pa(zo, 0, 1 - d)
-            sz[d, 4 - k, 1] = encode(other if k == 3 else other + decode(rz[d, 3 - k, 1]))
-            send(z_msg(d, k))
+            for chain in (0, 1):
+                own = pa(toward(d, k), 0, d if chain == 0 else 1 - d)
+                if k < 3 or chain == 0:
+                    own = own + decode(rz[d, 3 - k, chain])
+                sz[d, 4 - k, chain] = encode(own)
+                if k == 1:
+                    send(z_msg(d, k, chain))
+            if k > 1:
+                send(z_msg(d, k))
 
     def y_done(g):
         for d in (PLUS, MINUS):
@@ -220,9 +235,9 @@
             send(q_msg(d))
 
     def group(p):
-        if p == 0:
+        if p < 2:
             for yo in range(NY):
-                load(state_hbm, sbuf, 0, yo).wait()
+                (load(state_hbm, sbuf, 0, yo) if p else load_first(yo)).wait()
         multiply(p)
         if p == 0:
             pl.semaphore_wait(barrier, len(peers))
@@ -284,14 +299,14 @@
     for d in (PLUS, MINUS):
         q_msg(d).wait_recv()
     for h in (0, 1):
-        st[A:RANK, span(h)] = pb(0, 0, h) + decode(rraw2[1 - h, 1]) + decode(racc2[h])
+        st_out[A:RANK, span(h)] = pb(0, 0, h) + decode(rraw2[1 - h, 1]) + decode(racc2[h])
     for d in (PLUS, MINUS):
-        z_msg(d, 1).wait_recv()
+        for chain in (0, 1):
+            z_msg(d, 1, chain).wait_recv()
     for h in (0, 1):
-        st[0:A, span(h)] = pa(0, 0, h) + decode(rz[h, 3, 0]) + decode(rz[1 - h, 3, 1])
-
-    sk = st[...]
-    st_out[...] = sk
+        st_out[0:A, span(h)] = pa(0, 0, h) + decode(rz[h, 3, 0]) + decode(rz[1 - h, 3, 1])
+
+    sk = st_out[...]
     gpart[...] = lax.dot_general(sk, sk, (((1,), (1,)), ((), ())),
                                  precision=lax.Precision.HIGHEST, preferred_element_type=F32)
     gr = RANK // NC
@@ -378,13 +393,13 @@
         in_specs=[hbm, hbm, hbm],
         out_specs=(vmem, vmem, vmem),
         scratch_shapes=[
-            bf(STEPS, RANK), bf(RANK, STEPS), bf(NY, STEPS, NZ * OWN), bf(NY, 256, NZ * OWN), fl(NZ, NY, RANK, OWN), fl(256, 256),
+            bf(STEPS, RANK), bf(RANK, STEPS), bf(NY, STEPS, OWN), bf(NY, STEPS, NZ * OWN), bf(NY, 256, NZ * OWN), fl(NZ, NY, RANK, OWN), fl(256, 256),
             bf(2, NZ, 2, A, HALF), bf(2, NZ, 2, A, HALF), bf(2, NZ, A, HALF), bf(2, NZ, A, HALF),
             bf(2, 4, 2, A, HALF), bf(2, 4, 2, A, HALF), bf(2, 4, 2, NY, B, HALF), bf(2, 4, 2, NY, B, HALF),
             bf(2, 2, B, HALF), bf(2, 2, B, HALF), bf(2, B, HALF), bf(2, B, HALF),
             fl(7, 32, 256), fl(256, 256),
-            fl(RANK, OWN), fl(RANK, RANK), fl(7, 16, RANK), fl(NY, 16, RANK), fl(NZ, 16, RANK), fl(RANK, RANK),
-            dma((2, NY)), dma((2, 2, 5)), dma((2, 2, 5)), dma((2, 2, 4)), dma((2, 2, 4, 2)), dma((2, 2)), dma((2, 2)),
+            fl(RANK, RANK), fl(7, 16, RANK), fl(NY, 16, RANK), fl(NZ, 16, RANK), fl(RANK, RANK),
+            dma((3, NY)), dma((2, 2, 5)), dma((2, 2, 5)), dma((2, 2, 4, 2)), dma((2, 2, 4, 2)), dma((2, 2)), dma((2, 2)),
             dma((2, 7)), dma((2, NC)),
             dma((7,)), dma((7,)), dma((3,)), dma((NY,)), dma((7,)), dma((NZ,)), dma((7,)), dma((NC,)), dma((4,)),
         ],
@@ -442,12 +457,15 @@
     store.start()
     w = [gram[8 * b:8 * b + 8] for b in range(RANK // 8)]
     w_ref[...] = inverse_factor(w, scale)
-    basis[...] = lax.dot_general(st[...], w_ref[...], (((0,), (1,)), ((), ())),
-                                 precision=lax.Precision.HIGHEST, preferred_element_type=F32)
-    out = pltpu.make_async_copy(basis, out_hbm, sem.at[1])
-    out.start()
+    outs = []
+    for h in (0, 1):
+        basis[span(h)] = lax.dot_general(st[:, span(h)], w_ref[...], (((0,), (1,)), ((), ())),
+                                         precision=lax.Precision.HIGHEST, preferred_element_type=F32)
+        outs.append(pltpu.make_async_copy(basis.at[span(h)], out_hbm.at[span(h)], sem.at[1 + h]))
+        outs[h].start()
     store.wait()
-    out.wait()
+    for out in outs:
+        out.wait()
 
 
 def factor(gram, st, cor, scale):
@@ -459,7 +477,7 @@
         out_shape=(jax.ShapeDtypeStruct((OWN, RANK), F32), jax.ShapeDtypeStruct(cor.shape, F32)),
         in_specs=[vmem, vmem, vmem],
         out_specs=(hbm, hbm),
-        scratch_shapes=[pltpu.VMEM((OWN, RANK), F32), pltpu.VMEM((RANK, RANK), F32), pltpu.SemaphoreType.DMA((2,))],
+        scratch_shapes=[pltpu.VMEM((OWN, RANK), F32), pltpu.VMEM((RANK, RANK), F32), pltpu.SemaphoreType.DMA((3,))],
         compiler_params=pltpu.CompilerParams(vmem_limit_bytes=32 << 20),
     )(gram, st, cor)
 

time: 66.4 us -> 67.4 us (1.015)
  Pallas kernels: 65.7 us -> 66.7 us
    pallas_call x1, Pallas kernels: 60.2 us -> 61.3 us  [gather(): pl.pallas_call(gather_kernel, name='sketch_sums', out_shape=(pltpu.VMEM((...]
where the time goes in v5:
time: 67.4 us
  Pallas kernels  66.7 us (99%)
    pallas_call x1, Pallas kernels, gather(): pl.pallas_call(gather_kernel, name='sketch_sums', out_shape=(pltpu.VMEM((...  61.3 us
    pallas_call x1, Pallas kernels, factor(): pl.pallas_call(functools.partial(factor_kernel, scale), name='factor', ou...  5.42 us

profile of v5, /device:TPU:1, one launch (start us, length us, event | category | flops | bytes accessed | tf_op | source)
XLA Modules:
  0.0 67.4 jit_solution(8877974765716895642)
XLA Ops:
  0.6 61.3 %sketch_sums.1 = (f32[128,512]{1,0:T(8,128)S(1)}, f32[128,128]{1,0:T(8,128)S(1)}, f32[256,256]{1,0:T(8,128)S(1)}) custom-call(bf16[256,16384]{1,0:T(8,128)(2,1)} %state_hbm.1, bf16[256,128]{1,0:T(8,128)(2,1)} %r_hbm.1, bf16[256,16384]{1,0:T(8,128)(2,1)} %c_hbm.1), custom_call_target="tpu_custom_call" | custom-call | tf_op jit(solution)/shard_map/sketch_sums/pallas_call | solution.py:389
  61.9 5.4 %factor.1 = (f32[512,128]{1,0:T(8,128)}, f32[256,256]{1,0:T(8,128)}) custom-call(f32[128,128]{1,0:T(8,128)S(1)} %get-tuple-element.5.gram, f32[128,512]{1,0:T(8,128)S(1)} %get-tuple-element.6.st, f32[256,256]{1,0:T(8,128)S(1)} %get-tuple-element.7.cor), custom_call_target="tpu_custom_call" | custom-call | tf_op jit(solution)/shard_map/factor/pallas_call | solution.py:474

commit v6 on v4

--- a/solution.py
+++ b/solution.py
@@ -45,7 +45,7 @@
 def gather_kernel(state_hbm, r_hbm, c_hbm, st_out, gram_out, cor_out,
                   rbuf, rt, sbuf, cbuf, part, cor,
                   sraw, rraw, sacc, racc, sz, rz, sb, rb, sraw2, rraw2, sacc2, racc2, crecv, cfull,
-                  st, gpart, g1, g2, g3, g4,
+                  gpart, g1, g2, g3, g4,
                   load_sem, sem_raw, sem_acc, sem_z, sem_b, sem_raw2, sem_acc2,
                   sc, rc, sg1, rg1, sg2, rg2, sg3, rg3, sg4, rg4, out_sem):
     c, t = lax.axis_index("cell"), lax.axis_index("tm")
@@ -284,14 +284,13 @@
     for d in (PLUS, MINUS):
         q_msg(d).wait_recv()
     for h in (0, 1):
-        st[A:RANK, span(h)] = pb(0, 0, h) + decode(rraw2[1 - h, 1]) + decode(racc2[h])
+        st_out[A:RANK, span(h)] = pb(0, 0, h) + decode(rraw2[1 - h, 1]) + decode(racc2[h])
     for d in (PLUS, MINUS):
         z_msg(d, 1).wait_recv()
     for h in (0, 1):
-        st[0:A, span(h)] = pa(0, 0, h) + decode(rz[h, 3, 0]) + decode(rz[1 - h, 3, 1])
-
-    sk = st[...]
-    st_out[...] = sk
+        st_out[0:A, span(h)] = pa(0, 0, h) + decode(rz[h, 3, 0]) + decode(rz[1 - h, 3, 1])
+
+    sk = st_out[...]
     gpart[...] = lax.dot_general(sk, sk, (((1,), (1,)), ((), ())),
                                  precision=lax.Precision.HIGHEST, preferred_element_type=F32)
     gr = RANK // NC
@@ -383,7 +382,7 @@
             bf(2, 4, 2, A, HALF), bf(2, 4, 2, A, HALF), bf(2, 4, 2, NY, B, HALF), bf(2, 4, 2, NY, B, HALF),
             bf(2, 2, B, HALF), bf(2, 2, B, HALF), bf(2, B, HALF), bf(2, B, HALF),
             fl(7, 32, 256), fl(256, 256),
-            fl(RANK, OWN), fl(RANK, RANK), fl(7, 16, RANK), fl(NY, 16, RANK), fl(NZ, 16, RANK), fl(RANK, RANK),
+            fl(RANK, RANK), fl(7, 16, RANK), fl(NY, 16, RANK), fl(NZ, 16, RANK), fl(RANK, RANK),
             dma((2, NY)), dma((2, 2, 5)), dma((2, 2, 5)), dma((2, 2, 4)), dma((2, 2, 4, 2)), dma((2, 2)), dma((2, 2)),
             dma((2, 7)), dma((2, NC)),
             dma((7,)), dma((7,)), dma((3,)), dma((NY,)), dma((7,)), dma((NZ,)), dma((7,)), dma((NC,)), dma((4,)),
@@ -431,9 +430,8 @@
                 for i in range(j):
                     v = v - q[i] * l[j][i]
                 q.append(v)
-            for j in range(8):
-                new = new - (q[j] * inv[j]) * rows[j]
-            w[rb] = new
+            t = [(q[j] * inv[j]) * rows[j] for j in range(8)]
+            w[rb] = new - (((t[0] + t[1]) + (t[2] + t[3])) + ((t[4] + t[5]) + (t[6] + t[7])))
     return jnp.concatenate(out, axis=0)
 
 

time: 66.4 us -> 66.3 us (level)
  no operation moved by 1% of the time
where the time goes in v6:
time: 66.3 us; the launch traced here: 66.2 us
  Pallas kernels  65.6 us (99%)
    pallas_call x1, Pallas kernels, gather(): pl.pallas_call(gather_kernel, name='sketch_sums', out_shape=(pltpu.VMEM((...  60.2 us
    pallas_call x1, Pallas kernels, factor(): pl.pallas_call(functools.partial(factor_kernel, scale), name='factor', ou...  5.33 us

profile of v6, /device:TPU:1, one launch (start us, length us, event | category | flops | bytes accessed | tf_op | source)
XLA Modules:
  0.0 66.2 jit_solution(12755684596838153244)
XLA Ops:
  0.6 60.2 %sketch_sums.1 = (f32[128,512]{1,0:T(8,128)S(1)}, f32[128,128]{1,0:T(8,128)S(1)}, f32[256,256]{1,0:T(8,128)S(1)}) custom-call(bf16[256,16384]{1,0:T(8,128)(2,1)} %state_hbm.1, bf16[256,128]{1,0:T(8,128)(2,1)} %r_hbm.1, bf16[256,16384]{1,0:T(8,128)(2,1)} %c_hbm.1), custom_call_target="tpu_custom_call" | custom-call | tf_op jit(solution)/shard_map/sketch_sums/pallas_call | solution.py:373
  60.9 5.3 %factor.1 = (f32[512,128]{1,0:T(8,128)}, f32[256,256]{1,0:T(8,128)}) custom-call(f32[128,128]{1,0:T(8,128)S(1)} %get-tuple-element.5.gram, f32[128,512]{1,0:T(8,128)S(1)} %get-tuple-element.6.st, f32[256,256]{1,0:T(8,128)S(1)} %get-tuple-element.7.cor), custom_call_target="tpu_custom_call" | custom-call | tf_op jit(solution)/shard_map/factor/pallas_call | solution.py:454

commit v7 on v6

--- a/solution.py
+++ b/solution.py
@@ -440,12 +440,15 @@
     store.start()
     w = [gram[8 * b:8 * b + 8] for b in range(RANK // 8)]
     w_ref[...] = inverse_factor(w, scale)
-    basis[...] = lax.dot_general(st[...], w_ref[...], (((0,), (1,)), ((), ())),
-                                 precision=lax.Precision.HIGHEST, preferred_element_type=F32)
-    out = pltpu.make_async_copy(basis, out_hbm, sem.at[1])
-    out.start()
+    outs = []
+    for h in (0, 1):
+        basis[span(h)] = lax.dot_general(st[:, span(h)], w_ref[...], (((0,), (1,)), ((), ())),
+                                         precision=lax.Precision.HIGHEST, preferred_element_type=F32)
+        outs.append(pltpu.make_async_copy(basis.at[span(h)], out_hbm.at[span(h)], sem.at[1 + h]))
+        outs[h].start()
     store.wait()
-    out.wait()
+    for out in outs:
+        out.wait()
 
 
 def factor(gram, st, cor, scale):
@@ -457,7 +460,7 @@
         out_shape=(jax.ShapeDtypeStruct((OWN, RANK), F32), jax.ShapeDtypeStruct(cor.shape, F32)),
         in_specs=[vmem, vmem, vmem],
         out_specs=(hbm, hbm),
-        scratch_shapes=[pltpu.VMEM((OWN, RANK), F32), pltpu.VMEM((RANK, RANK), F32), pltpu.SemaphoreType.DMA((2,))],
+        scratch_shapes=[pltpu.VMEM((OWN, RANK), F32), pltpu.VMEM((RANK, RANK), F32), pltpu.SemaphoreType.DMA((3,))],
         compiler_params=pltpu.CompilerParams(vmem_limit_bytes=32 << 20),
     )(gram, st, cor)
 

time: 66.3 us -> 66.3 us (level)
  no operation moved by 1% of the time
where the time goes in v7:
time: 66.3 us; the launch traced here: 66.2 us
  Pallas kernels  65.6 us (99%)
    pallas_call x1, Pallas kernels, gather(): pl.pallas_call(gather_kernel, name='sketch_sums', out_shape=(pltpu.VMEM((...  60.2 us
    pallas_call x1, Pallas kernels, factor(): pl.pallas_call(functools.partial(factor_kernel, scale), name='factor', ou...  5.35 us

profile of v7, /device:TPU:1, one launch (start us, length us, event | category | flops | bytes accessed | tf_op | source)
XLA Modules:
  0.0 66.2 jit_solution(11861924446406959293)
XLA Ops:
  0.6 60.2 %sketch_sums.1 = (f32[128,512]{1,0:T(8,128)S(1)}, f32[128,128]{1,0:T(8,128)S(1)}, f32[256,256]{1,0:T(8,128)S(1)}) custom-call(bf16[256,16384]{1,0:T(8,128)(2,1)} %state_hbm.1, bf16[256,128]{1,0:T(8,128)(2,1)} %r_hbm.1, bf16[256,16384]{1,0:T(8,128)(2,1)} %c_hbm.1), custom_call_target="tpu_custom_call" | custom-call | tf_op jit(solution)/shard_map/sketch_sums/pallas_call | solution.py:373
  60.9 5.4 %factor.1 = (f32[512,128]{1,0:T(8,128)}, f32[256,256]{1,0:T(8,128)}) custom-call(f32[128,128]{1,0:T(8,128)S(1)} %get-tuple-element.5.gram, f32[128,512]{1,0:T(8,128)S(1)} %get-tuple-element.6.st, f32[256,256]{1,0:T(8,128)S(1)} %get-tuple-element.7.cor), custom_call_target="tpu_custom_call" | custom-call | tf_op jit(solution)/shard_map/factor/pallas_call | solution.py:457
